TPU v7x, 32 devices: a whole 2x2x4 slice. The times are simulated.
32 devices in a mesh: tower: 2 (over x), member: 16 (over z, y, core).
Axes of the slice: x: 2, y: 2, z: 4, core: 2. Of those that a mesh axis runs over, the one named last changes fastest.
Arguments:
- features: bfloat16 [4, 8192, 64], P('tower', 'member'), may hold values from -6 to 6
- compress: bfloat16 [4, 8192, 256], P('tower', 'member'), may hold values from -0.0625 to 0.0625
- top_down: bfloat16 [1024, 256], replicated, may hold values from -0.1875 to 0.1875
- top_up: bfloat16 [1024, 256], replicated, may hold values from -0.375 to 0.375
- top_bias: float32 [1024], replicated, may hold values from -3 to 3
- out_weight: bfloat16 [1024], replicated, may hold values from -0.1875 to 0.1875
- labels: int32 [64], replicated, may hold values 0 or 1
Outputs:
- grad_compress: float32 [4, 8192, 256], P('tower', 'member')
- grad_features: bfloat16 [4, 8192, 64], P('tower', 'member')
- grad_down: float32 [1024, 256], P(('tower', 'member'))
- grad_up: float32 [1024, 256], P(('tower', 'member'))
- grad_vectors: float32 [2, 1024], P(None, ('tower', 'member'))
All inputs are finite; a program needn't handle non-finite values.
Results may differ from a plain program's by a relative error of at most 0.0075.
Values may be sent and summed in bfloat16 or wider, within the bound.
No kernel may reach another device: no remote copies, remote signals or barrier semaphores. Data moves between devices by JAX's collectives and lax.ppermute only.
A program may use at most 64 MiB of HBM per device.

v0:
```python
import jax
import jax.numpy as jnp
from jax import lax
from jax.sharding import PartitionSpec as P


def contract_rows(left, right):
    return lax.dot_general(
        left, right, (((0,), (0,)), ((), ())), preferred_element_type=jnp.float32
    )


def cross_top(compressed, down, upper, bias, wout, target, sum_low, sum_score, sum_back):
    lowrank = sum_low(jnp.dot(compressed, down, preferred_element_type=jnp.float32)).astype(
        jnp.bfloat16
    )
    gate = (
        lax.dot_general(
            lowrank, upper, (((1,), (1,)), ((), ())), preferred_element_type=jnp.float32
        )
        + bias
    )
    comp_f = compressed.astype(jnp.float32)
    crossed = comp_f * gate + comp_f
    wide_out = wout.astype(jnp.float32)
    logit = sum_score(jnp.sum(crossed * wide_out[None, :], axis=1))
    dlogit = jax.nn.sigmoid(logit) - target
    dcrossed = dlogit[:, None] * wide_out[None, :]
    dgate_f = dcrossed * comp_f
    vectors = jnp.stack([jnp.sum(dgate_f, axis=0), jnp.sum(dlogit[:, None] * crossed, axis=0)])
    dgate = dgate_f.astype(jnp.bfloat16)
    grad_up = contract_rows(dgate, lowrank)
    dlowrank = sum_back(jnp.dot(dgate, upper, preferred_element_type=jnp.float32)).astype(
        jnp.bfloat16
    )
    grad_down = contract_rows(compressed, dlowrank)
    dcomp = dcrossed * (gate + 1.0) + lax.dot_general(
        dlowrank, down, (((1,), (1,)), ((), ())), preferred_element_type=jnp.float32
    )
    return (dcomp.astype(jnp.bfloat16), grad_down, grad_up, vectors)


def shards(features, compress, top_down, top_up, top_bias, out_weight, labels):
    local_towers, feat_rows, batch = features.shape
    comp_width = compress.shape[2]
    group_width = local_towers * comp_width
    mine = batch // lax.axis_size("member")
    member_idx = lax.axis_index("member")
    tower_idx = lax.axis_index("tower")
    block = features
    term = jnp.einsum("kfn,kfc->nkc", block, compress, preferred_element_type=jnp.float32)
    local = lax.psum_scatter(
        term.reshape(mine * lax.axis_size("member"), group_width),
        "member",
        scatter_dimension=0,
        tiled=True,
    ).astype(jnp.bfloat16)
    offset = tower_idx * group_width
    down_t = lax.dynamic_slice_in_dim(top_down, offset, group_width, 0)
    upper_t = lax.dynamic_slice_in_dim(top_up, offset, group_width, 0)
    bias_t = lax.dynamic_slice_in_dim(top_bias, offset, group_width, 0)
    wout_t = lax.dynamic_slice_in_dim(out_weight, offset, group_width, 0)
    target = lax.dynamic_slice_in_dim(labels, member_idx * mine, mine, 0).astype(jnp.float32)
    dcomp, grad_down, grad_up, vectors = cross_top(
        local,
        down_t,
        upper_t,
        bias_t,
        wout_t,
        target,
        lambda value: lax.psum(value, "tower"),
        lambda value: lax.psum(value, "tower"),
        lambda value: lax.psum(value, "tower"),
    )
    grad_down, grad_up, vectors = (
        lax.psum_scatter(grad_down, "member", scatter_dimension=0, tiled=True),
        lax.psum_scatter(grad_up, "member", scatter_dimension=0, tiled=True),
        lax.psum_scatter(vectors, "member", scatter_dimension=1, tiled=True),
    )
    piece = lax.all_gather(dcomp, "member", axis=0, tiled=True)
    count = piece.shape[0]
    block = features
    split_piece = piece.reshape(count, local_towers, comp_width)
    grad_w = jnp.einsum("kfn,nkc->kfc", block, split_piece, preferred_element_type=jnp.float32)
    column = jnp.einsum("kfc,nkc->kfn", compress, split_piece, preferred_element_type=jnp.float32)
    grad_x = column
    grad_w, grad_x = (grad_w, grad_x)
    return (grad_w, grad_x.astype(jnp.bfloat16), grad_down, grad_up, vectors)


def solution(mesh):
    placed = (P("tower", "member", None), P("tower", "member", None), P(), P(), P(), P(), P())
    return jax.shard_map(
        shards,
        mesh=mesh,
        in_specs=placed,
        out_specs=(
            P("tower", "member", None),
            P("tower", "member", None),
            P(("tower", "member"), None),
            P(("tower", "member"), None),
            P(None, ("tower", "member")),
        ),
        check_vma=False,
    )
```

profile of v0, /device:TPU:0, one launch (start us, length us, event | category | flops | bytes accessed | tf_op | source)
XLA Modules:
  0.0 264.3 jit_solution(413290777897398088)
XLA Ops:
  7.2 0.0 reduce-scatter.10.cloned.1.call-start
  7.3 0.7 copy-done.5
  8.0 0.1 dynamic-slice_convert_fusion.1
  8.0 0.1 dynamic_slice.17
  8.1 0.1 copy-done
  8.2 1.2 convolution_bitcast_fusion.1
  9.4 63.9 %all-reduce.2 = bf16[64,512]{1,0:T(8,128)(2,1)S(1)} all-reduce(f32[64,512]{1,0:T(8,128)S(1)} %bitcast.24), channel_id=2, replica_groups=mesh['tower'=2,'member'=16] {'member'}, use_global_device_ids=true, to_apply=%region_0.0.clone | all-reduce | flops 32768 | bytes 196608
  73.4 0.6 dynamic-slice
  74.6 0.2 fusion.7
  74.8 4.9 %psum.21 = bf16[4,256]{1,0:T(4,128)(2,1)S(1)} all-reduce(f32[4,256]{1,0:T(4,128)S(1)} %fusion.7), channel_id=1, replica_groups=mesh['tower'=2,'member'=16] {'tower'}, use_global_device_ids=true, to_apply=%region_1.0 | all-reduce | flops 1024 | bytes 6144 | tf_op jit(solution)/shard_map/psum | solution.py:71
  79.7 0.3 multiply_reduce_fusion.1
  80.0 4.9 %psum.22 = f32[4]{0:T(128)S(1)} all-reduce(f32[4]{0:T(128)S(1)} %get-tuple-element.27), channel_id=1, replica_groups=mesh['tower'=2,'member'=16] {'tower'}, use_global_device_ids=true, to_apply=%region_3.0 | all-reduce | flops 4 | bytes 32 | tf_op jit(solution)/shard_map/psum | solution.py:72
  84.9 0.7 copy-done.6
  85.6 0.1 divide_subtract_fusion
  85.7 0.1 fusion.11
  85.8 0.9 copy.25
  86.6 0.0 reduce-scatter.10.cloned.1.call-update
  86.7 0.0 reduce-scatter.8.cloned.1.call-start
  86.7 1.2 fusion.16
  87.9 0.0 reduce-scatter.6.cloned.1.call-start
  88.0 0.2 fusion.3
  88.1 4.9 %psum.23 = bf16[4,256]{1,0:T(4,128)(2,1)S(1)} all-reduce(f32[4,256]{1,0:T(4,128)S(1)} %fusion.3), channel_id=1, replica_groups=mesh['tower'=2,'member'=16] {'tower'}, use_global_device_ids=true, to_apply=%region_4.0 | all-reduce | flops 1024 | bytes 6144 | tf_op jit(solution)/shard_map/psum | solution.py:73
  93.1 1.1 fusion.25
  94.2 0.2 fusion.2
  94.3 17.4 %all-gather = bf16[16,4,512]{2,1,0:T(4,128)(2,1)S(1)} all-gather(bf16[1,4,512]{2,1,0:T(4,128)(2,1)S(1)} %fusion.2), channel_id=1, replica_groups=mesh['tower'=2,'member'=16] {'member'}, dimensions={0}, use_global_device_ids=true | all-gather | bytes 69632 | tf_op jit(solution)/shard_map/all_gather | solution.py:80
  111.8 0.3 convolution_bitcast_fusion
  112.2 1.3 copy.24
  113.5 0.9 fusion
  114.4 25.0 %reduce-scatter.10.cloned.1.call-done = f32[32,2]{1,0:T(8,128)} async-done(((f32[512,2]{1,0:T(8,128)}), f32[32,2]{1,0:T(8,128)}) %reduce-scatter.10.cloned.1.call-update) | async-done | bytes 272
  139.4 1.4 copy.26
  140.8 57.6 %reduce-scatter.8.cloned.1.call-done = f32[32,256]{1,0:T(8,128)} async-done(((f32[512,256]{1,0:T(8,128)}), f32[32,256]{1,0:T(8,128)}) %reduce-scatter.8.cloned.1.call-update) | async-done | bytes 32784 | tf_op jit(solution)/shard_map/reduce_scatter | solution.py:77
  198.4 59.3 %reduce-scatter.6.cloned.1.call-done = f32[32,256]{1,0:T(8,128)} async-done(((f32[512,256]{1,0:T(8,128)}), f32[32,256]{1,0:T(8,128)}) %reduce-scatter.6.cloned.1.call-update) | async-done | bytes 32784 | tf_op jit(solution)/shard_map/reduce_scatter | solution.py:76
  (18 shorter events, 0.1 us)
Async XLA Ops:
  7.2 1.1 copy-start
  7.2 132.2 %reduce-scatter.10.cloned.1.call-start = ((), (), s32[]{:S(2)}) async-start(), calls=%async_computation.5 | async-start | bytes 278528
  7.2 0.7 copy-start.5
  7.2 0.8 copy-start.4
  8.2 65.1 %copy-start.7 = (u32[32]{0:T(128)S(1)}, u32[32]{0:T(128)}, u32[]{:S(2)}) copy-start(u32[32]{0:T(128)} %constant.26) | copy-start | bytes 388
  8.2 66.4 %copy-start.2 = (bf16[1024,256]{1,0:T(8,128)(2,1)S(1)}, bf16[1024,256]{1,0:T(8,128)(2,1)}, u32[]{:S(2)}) copy-start(bf16[1024,256]{1,0:T(8,128)(2,1)} %param.9) | copy-start | bytes 1572868
  9.4 70.3 %copy-start.1 = (bf16[1024,256]{1,0:T(8,128)(2,1)S(1)}, bf16[1024,256]{1,0:T(8,128)(2,1)}, u32[]{:S(2)}) copy-start(bf16[1024,256]{1,0:T(8,128)(2,1)} %param.10) | copy-start | bytes 1572868
  84.9 0.7 copy-start.6
  86.7 111.7 %reduce-scatter.8.cloned.1.call-start = ((), (), s32[]{:S(2)}) async-start(), calls=%async_computation.4 | async-start | bytes 557056 | tf_op jit(solution)/shard_map/reduce_scatter | solution.py:77
  87.9 169.8 %reduce-scatter.6.cloned.1.call-start = ((), (), s32[]{:S(2)}) async-start(), calls=%async_computation.3 | async-start | bytes 557056 | tf_op jit(solution)/shard_map/reduce_scatter | solution.py:76
  94.3 17.5 %copy-start.3 = (bf16[2,512,64]{1,2,0:T(8,128)(2,1)S(1)}, bf16[2,512,64]{1,2,0:T(8,128)(2,1)}, u32[]{:S(2)}) copy-start(bf16[2,512,64]{1,2,0:T(8,128)(2,1)} %param.7) | copy-start | bytes 393220
Sparse Core Ops, SparseCore 0:
  86.8 52.5 reduce-scatter.9
  143.5 54.8 reduce-scatter.7
  203.0 54.7 reduce-scatter.5
where the time goes:
time: 265 us; the launch traced here: 264 us
  waiting for transfers between devices  142 us (54%)
  blocking collectives  96.1 us (36%)
  between operations  14.5 us (5%)
  local copies, waits for them, and re-layouts  5.76 us (2%)
  matrix products  5.49 us (2%)
    unnamed x1, blocking collectives  63.9 us
    reduce_scatter x1, waiting for transfers between devices, shards(): lax.psum_scatter(grad_down, 'member', scatter_dimension=0, tiled=True)  59.3 us
    reduce_scatter x1, waiting for transfers between devices, shards(): lax.psum_scatter(grad_up, 'member', scatter_dimension=0, tiled=True)  57.6 us
    unnamed x4, waiting for transfers between devices  25.1 us
    all_gather x1, blocking collectives, shards(): piece = lax.all_gather(dcomp, 'member', axis=0, tiled=True)  17.4 us
    psum x3, blocking collectives, shards(): lax.psum(value, 'tower')  14.8 us
    unnamed x20, local copies, waits for them, and re-layouts  5.64 us
  transfers between devices with their start and end apart: 3, of which 3 were waited for; matrix products, arithmetic and copies ran while one was open for 2% of the time, Pallas kernels for 0%

commit v1 on v0

--- a/solution.py
+++ b/solution.py
@@ -40,7 +40,7 @@
     return (dcomp.astype(jnp.bfloat16), grad_down, grad_up, vectors)
 
 
-def shards(features, compress, top_down, top_up, top_bias, out_weight, labels):
+def shards_spread(features, compress, top_down, top_up, top_bias, out_weight, labels):
     local_towers, feat_rows, batch = features.shape
     comp_width = compress.shape[2]
     group_width = local_towers * comp_width
@@ -88,7 +88,88 @@
     return (grad_w, grad_x.astype(jnp.bfloat16), grad_down, grad_up, vectors)
 
 
+def nt(left, right):
+    return lax.dot_general(
+        left, right, (((1,), (1,)), ((), ())), preferred_element_type=jnp.float32
+    )
+
+
+def exchange(value, tower_bit, member_bit):
+    towers, members = lax.axis_size("tower"), lax.axis_size("member")
+    pairs = [
+        (t * members + m, (t ^ tower_bit) * members + (m ^ member_bit))
+        for t in range(towers)
+        for m in range(members)
+    ]
+    return lax.ppermute(value, ("tower", "member"), pairs)
+
+
+def shards_doubling(features, compress, top_down, top_up, top_bias, out_weight, labels):
+    local_towers, feat_rows, batch = features.shape
+    comp_width = compress.shape[2]
+    members = lax.axis_size("member")
+    half = local_towers // 2
+    member_idx = lax.axis_index("member")
+    tower_idx = lax.axis_index("tower")
+    side = member_idx % 2
+    term = jnp.einsum("kfn,kfc->knc", features, compress, preferred_element_type=jnp.float32)
+    kept = lax.dynamic_slice_in_dim(term, side * half, half, 0)
+    sent = lax.dynamic_slice_in_dim(term, (1 - side) * half, half, 0)
+    total = kept + exchange(sent, 0, 1)
+    stride = 2
+    while stride < members:
+        total = total + exchange(total, 0, stride)
+        stride *= 2
+    mine = total.astype(jnp.bfloat16)
+    pieces = {
+        (t, s): mine if (t, s) == (0, 0) else exchange(mine, t, s) for t in (0, 1) for s in (0, 1)
+    }
+    by_side = []
+    for t in (0, 1):
+        near, far = pieces[t, 0], pieces[t, 1]
+        by_side.append(
+            jnp.concatenate([jnp.where(side == 0, near, far), jnp.where(side == 0, far, near)], 0)
+        )
+    parts = jnp.concatenate(
+        [
+            jnp.where(tower_idx == 0, by_side[0], by_side[1]),
+            jnp.where(tower_idx == 0, by_side[1], by_side[0]),
+        ],
+        0,
+    )
+    compressed = jnp.transpose(parts, (1, 0, 2)).reshape(batch, -1)
+    lowrank = jnp.dot(compressed, top_down, preferred_element_type=jnp.float32).astype(jnp.bfloat16)
+    gate = nt(lowrank, top_up) + top_bias
+    comp_f = compressed.astype(jnp.float32)
+    crossed = comp_f * gate + comp_f
+    wide_out = out_weight.astype(jnp.float32)
+    logit = jnp.sum(crossed * wide_out[None, :], axis=1)
+    dlogit = jax.nn.sigmoid(logit) - labels.astype(jnp.float32)
+    dcrossed = dlogit[:, None] * wide_out[None, :]
+    dgate_f = dcrossed * comp_f
+    vectors = jnp.stack([jnp.sum(dgate_f, axis=0), jnp.sum(dlogit[:, None] * crossed, axis=0)])
+    dgate = dgate_f.astype(jnp.bfloat16)
+    dlowrank = jnp.dot(dgate, top_up, preferred_element_type=jnp.float32).astype(jnp.bfloat16)
+    width = compressed.shape[1] // (2 * members)
+    column = (tower_idx * members + member_idx) * width
+    own = lambda value: lax.dynamic_slice_in_dim(value, column, width, 1)
+    grad_up = contract_rows(own(dgate), lowrank)
+    grad_down = contract_rows(own(compressed), dlowrank)
+    group = local_towers * comp_width
+    block = lambda value, dim: lax.dynamic_slice_in_dim(value, tower_idx * group, group, dim)
+    dcomp = (
+        block(dcrossed, 1) * (block(gate, 1) + 1.0) + nt(dlowrank, block(top_down, 0))
+    ).astype(jnp.bfloat16)
+    dparts = dcomp.reshape(batch, local_towers, comp_width)
+    grad_w = jnp.einsum("kfn,nkc->kfc", features, dparts, preferred_element_type=jnp.float32)
+    grad_x = jnp.einsum("kfc,nkc->kfn", compress, dparts, preferred_element_type=jnp.float32)
+    return (grad_w, grad_x.astype(jnp.bfloat16), grad_down, grad_up, own(vectors))
+
+
 def solution(mesh):
+    members = mesh.shape["member"]
+    small = mesh.shape["tower"] == 2 and members >= 2 and members & (members - 1) == 0
+    shards = shards_doubling if small else shards_spread
     placed = (P("tower", "member", None), P("tower", "member", None), P(), P(), P(), P(), P())
     return jax.shard_map(
         shards,

time: 265 us -> 33.3 us (0.13)
  waiting for transfers between devices: 142 us -> 11.1 us
  blocking collectives: 96.1 us -> 0 us
  between operations: 14.5 us -> 0.83 us
  starting transfers between devices: 0.12 us -> 10.5 us
    reduce_scatter x2 -> x0, waiting for transfers between devices: 117 us -> none  [the longest x1 59.3 us: shards(): lax.psum_scatter(grad_down, 'member', scatter_dimension=0, tiled=True)]
    unnamed x1 -> x0, blocking collectives: 63.9 us -> none
    unnamed x4 -> x0, waiting for transfers between devices: 25.1 us -> none
    all_gather x1 -> x0, blocking collectives: 17.4 us -> none  [shards(): piece = lax.all_gather(dcomp, 'member', axis=0, tiled=True)]
    psum x3 -> x0, blocking collectives: 14.8 us -> none  [shards(): lax.psum(value, 'tower')]
    ppermute x0 -> x7, waiting for transfers between devices: none -> 11.1 us  [exchange(): return lax.ppermute(value, ('tower', 'member'), pairs)]
    ppermute x0 -> x7, starting transfers between devices: none -> 10.5 us  [exchange(): return lax.ppermute(value, ('tower', 'member'), pairs)]
    unnamed x20 -> x16, local copies, waits for them, and re-layouts: 5.64 us -> 4.47 us
  transfers between devices with their start and end apart: 3 -> 7, of which waited for: 3 -> 6; matrix products, arithmetic and copies ran while one was open for 2% -> 0% of each run, Pallas kernels for 0% -> 0%
where the time goes in v1:
time: 33.3 us; the launch traced here: 33 us
  waiting for transfers between devices  11.1 us (33%)
  starting transfers between devices  10.5 us (32%)
  matrix products  5.12 us (15%)
  local copies, waits for them, and re-layouts  4.5 us (14%)
  other arithmetic  0.98 us (3%)
  between operations  0.83 us (2%)
    ppermute x7, waiting for transfers between devices, exchange(): return lax.ppermute(value, ('tower', 'member'), pairs)  11.1 us
    ppermute x7, starting transfers between devices, exchange(): return lax.ppermute(value, ('tower', 'member'), pairs)  10.5 us
    unnamed x16, local copies, waits for them, and re-layouts  4.47 us
    dot_general x2, matrix products, contract_rows(): lax.dot_general(left, right, (((0,), (0,)), ((), ())), preferred_element_...  1.73 us
    dot_general x1, matrix products, shards_doubling(): jnp.einsum('kfn,kfc->knc', features, compress, preferred_element_type=jnp...  1.1 us
    dot_general x1, matrix products, shards_doubling(): jnp.einsum('kfc,nkc->kfn', compress, dparts, preferred_element_type=jnp.f...  0.94 us
  transfers between devices with their start and end apart: 7, of which 6 were waited for; matrix products, arithmetic and copies ran while one was open for 0% of the time, Pallas kernels for 0%

profile of v1, /device:TPU:0, one launch (start us, length us, event | category | flops | bytes accessed | tf_op | source)
XLA Modules:
  0.0 33.0 jit_solution(13891935098296467514)
XLA Ops:
  0.6 0.0 copy-start
  0.7 1.0 %copy-done = bf16[2,512,256]{2,1,0:T(8,128)(2,1)S(1)} copy-done((bf16[2,512,256]{2,1,0:T(8,128)(2,1)S(1)}, bf16[2,512,256]{2,1,0:T(8,128)(2,1)}, u32[]{:S(2)}) %copy-start) | copy-done | bytes 524312
  1.7 1.1 %fusion.17 = f32[2,64,256]{2,1,0:T(8,128)S(1)} fusion(bf16[2,512,64]{1,2,0:T(8,128)(2,1)} %param.7, bf16[2,512,256]{2,1,0:T(8,128)(2,1)S(1)} %copy-done), kind=kOutput, calls=%fused_computation.44 | convolution fusion | flops 33554432 | bytes 786432 | tf_op jit(solution)/shard_map/kfn,kfc->knc/dot_general | solution.py:115
  2.8 0.5 %collective-permute-start = (f32[1,64,256]{2,1,0:T(8,128)S(1)}, f32[1,64,256]{2,1,0:T(8,128)S(1)}, u32[]{:S(2)}, u32[]{:S(2)}) collective-permute-start(f32[1,64,256]{2,1,0:T(8,128)S(1)} %constant_dynamic-slice_fusion), channel_id=1, source_target_pairs={{0,1},{1,0},{2,3},{3,2},{4,5},{5,4},{6,7},{7,6},{8,9},{9,8},{10,11... | collective-permute-start | bytes 196616 | tf_op jit(solution)/shard_map/ppermute | solution.py:104
  3.3 0.9 %collective-permute-done = f32[1,64,256]{2,1,0:T(8,128)S(1)} collective-permute-done((f32[1,64,256]{2,1,0:T(8,128)S(1)}, f32[1,64,256]{2,1,0:T(8,128)S(1)}, u32[]{:S(2)}, u32[]{:S(2)}) %collective-permute-start) | collective-permute-done | bytes 65568 | tf_op jit(solution)/shard_map/ppermute | solution.py:104
  4.2 2.9 %collective-permute-start.1 = (f32[1,64,256]{2,1,0:T(8,128)S(1)}, f32[1,64,256]{2,1,0:T(8,128)S(1)}, u32[]{:S(2)}, u32[]{:S(2)}) collective-permute-start(f32[1,64,256]{2,1,0:T(8,128)S(1)} %dynamic-slice_add_fusion), channel_id=1, source_target_pairs={{0,2},{1,3},{2,0},{3,1},{4,6},{5,7},{6,4},{7,5},{8,10},{9,11},{10,... | collective-permute-start | bytes 196616 | tf_op jit(solution)/shard_map/ppermute | solution.py:104
  7.2 2.4 %collective-permute-done.1 = f32[1,64,256]{2,1,0:T(8,128)S(1)} collective-permute-done((f32[1,64,256]{2,1,0:T(8,128)S(1)}, f32[1,64,256]{2,1,0:T(8,128)S(1)}, u32[]{:S(2)}, u32[]{:S(2)}) %collective-permute-start.1) | collective-permute-done | bytes 65568 | tf_op jit(solution)/shard_map/ppermute | solution.py:104
  9.6 2.0 %collective-permute-start.2 = (f32[1,64,256]{2,1,0:T(8,128)S(1)}, f32[1,64,256]{2,1,0:T(8,128)S(1)}, u32[]{:S(2)}, u32[]{:S(2)}) collective-permute-start(f32[1,64,256]{2,1,0:T(8,128)S(1)} %add.63), channel_id=1, source_target_pairs={{0,4},{1,5},{2,6},{3,7},{4,0},{5,1},{6,2},{7,3},{8,12},{9,13},{10,... | collective-permute-start | bytes 196616 | tf_op jit(solution)/shard_map/ppermute | solution.py:104
  11.6 2.4 %collective-permute-done.2 = f32[1,64,256]{2,1,0:T(8,128)S(1)} collective-permute-done((f32[1,64,256]{2,1,0:T(8,128)S(1)}, f32[1,64,256]{2,1,0:T(8,128)S(1)}, u32[]{:S(2)}, u32[]{:S(2)}) %collective-permute-start.2) | collective-permute-done | bytes 65568 | tf_op jit(solution)/shard_map/ppermute | solution.py:104
  14.0 3.0 %collective-permute-start.3 = (f32[1,64,256]{2,1,0:T(8,128)S(1)}, f32[1,64,256]{2,1,0:T(8,128)S(1)}, u32[]{:S(2)}, u32[]{:S(2)}) collective-permute-start(f32[1,64,256]{2,1,0:T(8,128)S(1)} %add.64), channel_id=1, source_target_pairs={{0,8},{1,9},{2,10},{3,11},{4,12},{5,13},{6,14},{7,15},{8,0},{9,1},... | collective-permute-start | bytes 196616 | tf_op jit(solution)/shard_map/ppermute | solution.py:104
  16.9 2.2 %collective-permute-done.3 = f32[1,64,256]{2,1,0:T(8,128)S(1)} collective-permute-done((f32[1,64,256]{2,1,0:T(8,128)S(1)}, f32[1,64,256]{2,1,0:T(8,128)S(1)}, u32[]{:S(2)}, u32[]{:S(2)}) %collective-permute-start.3) | collective-permute-done | bytes 65568 | tf_op jit(solution)/shard_map/ppermute | solution.py:104
  19.2 0.1 collective-permute-start.4
  19.3 0.7 %copy-done.4 = bf16[1024]{0:T(1024)(128)(2,1)S(1)} copy-done((bf16[1024]{0:T(1024)(128)(2,1)S(1)}, bf16[1024]{0:T(1024)(128)(2,1)}, u32[]{:S(2)}) %copy-start.4) | copy-done | bytes 2072
  20.0 1.9 %collective-permute-start.5 = (bf16[1,64,256]{2,1,0:T(8,128)(2,1)S(1)}, bf16[1,64,256]{2,1,0:T(8,128)(2,1)S(1)}, u32[]{:S(2)}, u32[]{:S(2)}) collective-permute-start(bf16[1,64,256]{2,1,0:T(8,128)(2,1)S(1)} %add_convert_fusion), channel_id=1, source_target_pairs={{0,16},{1,17},{2,18},{3,19},{4,20},{5,21},{6,22},{7,23},{8,24},{9,... | collective-permute-start | bytes 98312 | tf_op jit(solution)/shard_map/ppermute | solution.py:104
  21.9 0.2 collective-permute-start.6
  22.1 1.9 %collective-permute-done.5 = bf16[1,64,256]{2,1,0:T(8,128)(2,1)S(1)} collective-permute-done((bf16[1,64,256]{2,1,0:T(8,128)(2,1)S(1)}, bf16[1,64,256]{2,1,0:T(8,128)(2,1)S(1)}, u32[]{:S(2)}, u32[]{:S(2)}) %collective-permute-start.5) | collective-permute-done | bytes 32800 | tf_op jit(solution)/shard_map/ppermute | solution.py:104
  24.0 1.2 %collective-permute-done.6 = bf16[1,64,256]{2,1,0:T(8,128)(2,1)S(1)} collective-permute-done((bf16[1,64,256]{2,1,0:T(8,128)(2,1)S(1)}, bf16[1,64,256]{2,1,0:T(8,128)(2,1)S(1)}, u32[]{:S(2)}, u32[]{:S(2)}) %collective-permute-start.6) | collective-permute-done | bytes 32800 | tf_op jit(solution)/shard_map/ppermute | solution.py:104
  25.3 0.0 copy-start.5
  25.3 0.2 convolution_convert_fusion.2
  25.5 0.8 %copy-done.1 = bf16[1024,256]{1,0:T(8,128)(2,1)S(1)} copy-done((bf16[1024,256]{1,0:T(8,128)(2,1)S(1)}, bf16[1024,256]{1,0:T(8,128)(2,1)}, u32[]{:S(2)}) %copy-start.1) | copy-done | bytes 524312
  26.3 0.4 %multiply_reduce_fusion.2 = (f32[64]{0:T(128)S(1)}, f32[64,1024]{1,0:T(8,128)S(1)}) fusion(bf16[64,1024]{1,0:T(8,128)(2,1)S(1)} %bitcast.33, f32[1024]{0:T(1024)S(1)} %convert_element_type.36, f32[1024]{0:T(1024)S(1)} %copy-done.5, bf16[64,256]{1,0:T(8,128)(2,1)S(1)} %convolution_convert_fusion.2, bf16[1024,256]{1,0:T(8,128)(2,1)S(1)} %copy-done.1), kind=kOutput, calls=%fused_computation.14 | convolution fusion | flops 33947584 | bytes 958720 | tf_op jit(solution)/shard_map/dot_general | solution.py:92
  26.7 0.7 %copy-done.6 = s32[64]{0:T(128)S(1)} copy-done((s32[64]{0:T(128)S(1)}, s32[64]{0:T(128)}, u32[]{:S(2)}) %copy-start.6) | copy-done | bytes 280
  27.4 0.1 multiply_reduce_fusion
  27.5 0.2 convolution_convert_fusion.1
  27.7 0.9 %fusion.9 = f32[32,256]{1,0:T(8,128)} fusion(bf16[64,256]{1,0:T(8,128)(2,1)S(1)} %convolution_convert_fusion.2, bf16[64,1024]{1,0:T(8,128)(2,1)S(1)} %get-tuple-element.16, s32[]{:T(128)S(6)} %select_n.67), kind=kOutput, calls=%fused_computation.32 | convolution fusion | flops 1048576 | bytes 81924 | tf_op jit(solution)/shard_map/dot_general | solution.py:8
  28.6 0.9 %fusion.11 = f32[32,256]{1,0:T(8,128)} fusion(bf16[64,256]{1,0:T(8,128)(2,1)S(1)} %convolution_convert_fusion.1, bf16[64,1024]{1,0:T(8,128)(2,1)S(1)} %bitcast.35, s32[]{:T(128)S(6)} %select_n.67), kind=kOutput, calls=%fused_computation.34 | convolution fusion | flops 1048576 | bytes 81924 | tf_op jit(solution)/shard_map/dot_general | solution.py:8
  29.5 0.2 fusion.1
  29.7 0.9 %fusion = bf16[2,512,64]{1,2,0:T(8,128)(2,1)} fusion(bf16[2,512,256]{2,1,0:T(8,128)(2,1)S(1)} %copy-done, bf16[8,2,8,256]{3,2,1,0:T(8,128)(2,1)S(1)} %bitcast.36), kind=kOutput, calls=%fused_computation.3 | convolution fusion | flops 33619968 | bytes 720896 | tf_op jit(solution)/shard_map/kfc,nkc->kfn/dot_general | solution.py:165
  30.6 0.3 %convolution_bitcast_fusion = f32[2,512,256]{1,2,0:T(8,128)S(1)} fusion(bf16[2,512,64]{1,2,0:T(8,128)(2,1)S(1)} %copy-done.3, bf16[8,2,8,256]{3,2,1,0:T(8,128)(2,1)S(1)} %bitcast.37), kind=kOutput, calls=%fused_computation | convolution fusion | flops 33554432 | bytes 1245184 | tf_op jit(solution)/shard_map/kfn,nkc->kfc/dot_general | solution.py:164
  31.0 0.1 multiply_reduce_fusion.1
  31.1 1.3 %copy.18 = f32[2,512,256]{2,1,0:T(8,128)} copy(f32[2,512,256]{1,2,0:T(8,128)S(1)} %convolution_bitcast_fusion) | data formatting | bytes 2097152
  32.4 0.6 %fusion.16 = f32[2,32]{1,0:T(2,128)} fusion(s32[]{:T(128)S(6)} %select_n.67, f32[1,1024]{1,0:T(1,128)S(1)} %bitcast.40, f32[1,1024]{1,0:T(1,128)S(1)} %bitcast.38), kind=kLoop, calls=%fused_computation.42 | loop fusion | flops 64 | bytes 8452 | tf_op jit(solution)/shard_map/stack | solution.py:150
  (23 shorter events, 0.2 us)
Async XLA Ops:
  0.6 1.0 %copy-start = (bf16[2,512,256]{2,1,0:T(8,128)(2,1)S(1)}, bf16[2,512,256]{2,1,0:T(8,128)(2,1)}, u32[]{:S(2)}) copy-start(bf16[2,512,256]{2,1,0:T(8,128)(2,1)} %param.8) | copy-start | bytes 1572868
  2.8 1.4 %collective-permute-start = (f32[1,64,256]{2,1,0:T(8,128)S(1)}, f32[1,64,256]{2,1,0:T(8,128)S(1)}, u32[]{:S(2)}, u32[]{:S(2)}) collective-permute-start(f32[1,64,256]{2,1,0:T(8,128)S(1)} %constant_dynamic-slice_fusion), channel_id=1, source_target_pairs={{0,1},{1,0},{2,3},{3,2},{4,5},{5,4},{6,7},{7,6},{8,9},{9,8},{10,11... | collective-permute-start | bytes 196616 | tf_op jit(solution)/shard_map/ppermute | solution.py:104
  4.2 5.3 %collective-permute-start.1 = (f32[1,64,256]{2,1,0:T(8,128)S(1)}, f32[1,64,256]{2,1,0:T(8,128)S(1)}, u32[]{:S(2)}, u32[]{:S(2)}) collective-permute-start(f32[1,64,256]{2,1,0:T(8,128)S(1)} %dynamic-slice_add_fusion), channel_id=1, source_target_pairs={{0,2},{1,3},{2,0},{3,1},{4,6},{5,7},{6,4},{7,5},{8,10},{9,11},{10,... | collective-permute-start | bytes 196616 | tf_op jit(solution)/shard_map/ppermute | solution.py:104
  9.6 4.3 %collective-permute-start.2 = (f32[1,64,256]{2,1,0:T(8,128)S(1)}, f32[1,64,256]{2,1,0:T(8,128)S(1)}, u32[]{:S(2)}, u32[]{:S(2)}) collective-permute-start(f32[1,64,256]{2,1,0:T(8,128)S(1)} %add.63), channel_id=1, source_target_pairs={{0,4},{1,5},{2,6},{3,7},{4,0},{5,1},{6,2},{7,3},{8,12},{9,13},{10,... | collective-permute-start | bytes 196616 | tf_op jit(solution)/shard_map/ppermute | solution.py:104
  14.0 5.2 %collective-permute-start.3 = (f32[1,64,256]{2,1,0:T(8,128)S(1)}, f32[1,64,256]{2,1,0:T(8,128)S(1)}, u32[]{:S(2)}, u32[]{:S(2)}) collective-permute-start(f32[1,64,256]{2,1,0:T(8,128)S(1)} %add.64), channel_id=1, source_target_pairs={{0,8},{1,9},{2,10},{3,11},{4,12},{5,13},{6,14},{7,15},{8,0},{9,1},... | collective-permute-start | bytes 196616 | tf_op jit(solution)/shard_map/ppermute | solution.py:104
  19.2 2.8 %collective-permute-start.4 = (bf16[1,64,256]{2,1,0:T(8,128)(2,1)S(1)}, bf16[1,64,256]{2,1,0:T(8,128)(2,1)S(1)}, u32[]{:S(2)}, u32[]{:S(2)}) collective-permute-start(bf16[1,64,256]{2,1,0:T(8,128)(2,1)S(1)} %add_convert_fusion), channel_id=1, source_target_pairs={{0,1},{1,0},{2,3},{3,2},{4,5},{5,4},{6,7},{7,6},{8,9},{9,8},{10,11... | collective-permute-start | bytes 98312 | tf_op jit(solution)/shard_map/ppermute | solution.py:104
  19.3 0.7 %copy-start.4 = (bf16[1024]{0:T(1024)(128)(2,1)S(1)}, bf16[1024]{0:T(1024)(128)(2,1)}, u32[]{:S(2)}) copy-start(bf16[1024]{0:T(1024)(128)(2,1)} %param.12) | copy-start | bytes 6148
  20.0 5.3 %copy-start.2 = (bf16[1024,256]{1,0:T(8,128)(2,1)S(1)}, bf16[1024,256]{1,0:T(8,128)(2,1)}, u32[]{:S(2)}) copy-start(bf16[1024,256]{1,0:T(8,128)(2,1)} %param.9) | copy-start | bytes 1572868
  20.0 4.0 %collective-permute-start.5 = (bf16[1,64,256]{2,1,0:T(8,128)(2,1)S(1)}, bf16[1,64,256]{2,1,0:T(8,128)(2,1)S(1)}, u32[]{:S(2)}, u32[]{:S(2)}) collective-permute-start(bf16[1,64,256]{2,1,0:T(8,128)(2,1)S(1)} %add_convert_fusion), channel_id=1, source_target_pairs={{0,16},{1,17},{2,18},{3,19},{4,20},{5,21},{6,22},{7,23},{8,24},{9,... | collective-permute-start | bytes 98312 | tf_op jit(solution)/shard_map/ppermute | solution.py:104
  21.9 3.3 %collective-permute-start.6 = (bf16[1,64,256]{2,1,0:T(8,128)(2,1)S(1)}, bf16[1,64,256]{2,1,0:T(8,128)(2,1)S(1)}, u32[]{:S(2)}, u32[]{:S(2)}) collective-permute-start(bf16[1,64,256]{2,1,0:T(8,128)(2,1)S(1)} %add_convert_fusion), channel_id=1, source_target_pairs={{0,17},{1,16},{2,19},{3,18},{4,21},{5,20},{6,23},{7,22},{8,25},{9,... | collective-permute-start | bytes 98312 | tf_op jit(solution)/shard_map/ppermute | solution.py:104
  25.3 1.0 %copy-start.1 = (bf16[1024,256]{1,0:T(8,128)(2,1)S(1)}, bf16[1024,256]{1,0:T(8,128)(2,1)}, u32[]{:S(2)}) copy-start(bf16[1024,256]{1,0:T(8,128)(2,1)} %param.10) | copy-start | bytes 1572868
  25.3 1.0 %copy-start.5 = (f32[1024]{0:T(1024)S(1)}, f32[1024]{0:T(1024)}, u32[]{:S(2)}) copy-start(f32[1024]{0:T(1024)} %param.11) | copy-start | bytes 12292
  26.7 0.7 %copy-start.6 = (s32[64]{0:T(128)S(1)}, s32[64]{0:T(128)}, u32[]{:S(2)}) copy-start(s32[64]{0:T(128)} %param.13) | copy-start | bytes 772
  29.7 1.0 %copy-start.3 = (bf16[2,512,64]{1,2,0:T(8,128)(2,1)S(1)}, bf16[2,512,64]{1,2,0:T(8,128)(2,1)}, u32[]{:S(2)}) copy-start(bf16[2,512,64]{1,2,0:T(8,128)(2,1)} %param.7) | copy-start | bytes 393220

commit v2 on v0

--- a/solution.py
+++ b/solution.py
@@ -1,6 +1,10 @@
+import functools
+
 import jax
 import jax.numpy as jnp
 from jax import lax
+from jax.experimental import pallas as pl
+from jax.experimental.pallas import tpu as pltpu
 from jax.sharding import PartitionSpec as P
 
 
@@ -40,7 +44,7 @@
     return (dcomp.astype(jnp.bfloat16), grad_down, grad_up, vectors)
 
 
-def shards(features, compress, top_down, top_up, top_bias, out_weight, labels):
+def shards_spread(features, compress, top_down, top_up, top_bias, out_weight, labels):
     local_towers, feat_rows, batch = features.shape
     comp_width = compress.shape[2]
     group_width = local_towers * comp_width
@@ -88,6 +92,224 @@
     return (grad_w, grad_x.astype(jnp.bfloat16), grad_down, grad_up, vectors)
 
 
+F32, BF16 = jnp.float32, jnp.bfloat16
+VMEM = pl.BlockSpec(memory_space=pltpu.VMEM)
+ANY = pl.BlockSpec(memory_space=pl.ANY)
+CHUNKS = 4
+
+
+def nt(left, right):
+    return lax.dot_general(left, right, (((1,), (1,)), ((), ())), preferred_element_type=F32)
+
+
+def exchange(value, tower_bit, member_bit):
+    towers, members = lax.axis_size("tower"), lax.axis_size("member")
+    pairs = [
+        (t * members + m, (t ^ tower_bit) * members + (m ^ member_bit))
+        for t in range(towers)
+        for m in range(members)
+    ]
+    return lax.ppermute(value, ("tower", "member"), pairs)
+
+
+def term_kernel(flip, feat_hbm, comp_hbm, out, feat, comp, sems):
+    which = lax.rem(lax.axis_index("member") + flip, 2)
+    rows = comp.shape[1]
+    load_feat = pltpu.make_async_copy(feat_hbm.at[which], feat, sems.at[2])
+    loads = [
+        pltpu.make_async_copy(
+            comp_hbm.at[which, pl.ds(i * rows, rows)], comp.at[i], sems.at[i]
+        )
+        for i in range(2)
+    ]
+    load_feat.start()
+    for load in loads:
+        load.start()
+    load_feat.wait()
+    total = None
+    for i in range(2):
+        loads[i].wait()
+        part = jnp.dot(feat[:, i * rows : (i + 1) * rows], comp[i], preferred_element_type=F32)
+        total = part if total is None else total + part
+    out[...] = total
+
+
+def term(flip, feat_t, compress):
+    _, batch, rows = feat_t.shape
+    width = compress.shape[2]
+    return pl.pallas_call(
+        lambda *refs: term_kernel(flip, *refs),
+        out_shape=jax.ShapeDtypeStruct((batch, width), F32),
+        in_specs=[ANY, ANY],
+        out_specs=VMEM,
+        scratch_shapes=[
+            pltpu.VMEM((batch, rows), BF16),
+            pltpu.VMEM((2, rows // 2, width), BF16),
+            pltpu.SemaphoreType.DMA((3,)),
+        ],
+        compiler_params=pltpu.CompilerParams(vmem_limit_bytes=2 << 20),
+        cost_estimate=pl.CostEstimate(
+            flops=2 * batch * rows * width, bytes_accessed=2 * rows * (width + batch), transcendentals=0
+        ),
+    )(
+        pltpu.with_memory_space_constraint(feat_t, pltpu.HBM),
+        pltpu.with_memory_space_constraint(compress, pltpu.HBM),
+    )
+
+
+def top_kernel(
+    mine, side_piece, tower_piece, both_piece, down, upper, bias, wout, labels_hbm, feat, comp,
+    grad_w_hbm, grad_x, grad_down, grad_up, vectors,
+    compressed, gates, wide, labels, grad_w, square, sems,
+):
+    tower, member = lax.axis_index("tower"), lax.axis_index("member")
+    side = lax.rem(member, 2)
+    batch, width = mine.shape
+    pieces = compressed.shape[0]
+    load_labels = pltpu.make_async_copy(labels_hbm, labels, sems.at[CHUNKS])
+    load_labels.start()
+    compressed[2 * tower + side] = mine[...]
+    compressed[2 * tower + 1 - side] = side_piece[...]
+    compressed[2 * (1 - tower) + side] = tower_piece[...]
+    compressed[2 * (1 - tower) + 1 - side] = both_piece[...]
+    block = lambda j: slice(j * width, (j + 1) * width)
+    summed = lambda parts: functools.reduce(jnp.add, parts)
+
+    low = summed(
+        jnp.dot(compressed[j], down[block(j), :], preferred_element_type=F32)
+        for j in range(pieces)
+    ).astype(BF16)
+    weighted, scores = [], []
+    for j in range(pieces):
+        gate = nt(low, upper[block(j), :]) + bias[:, block(j)]
+        gates[j] = gate
+        out_row = wout[:, block(j)].astype(F32)
+        wide[j] = out_row
+        comp_f = compressed[j].astype(F32)
+        weighted.append((comp_f * out_row).astype(BF16))
+        scores.append((comp_f * gate + comp_f) * out_row)
+    logit = jnp.sum(summed(scores), axis=1, keepdims=True)
+    back = summed(
+        jnp.dot(weighted[j], upper[block(j), :], preferred_element_type=F32)
+        for j in range(pieces)
+    )
+    back_low = back.astype(BF16)
+    slopes = []
+    for k in range(2):
+        j = 2 * tower + k
+        rows = pl.ds(pl.multiple_of(j * width, width), width)
+        slopes.append(wide[j] * (gates[j] + 1.0) + nt(back_low, down[rows, :]))
+    row = lax.broadcasted_iota(jnp.int32, (batch, batch), 0)
+    col = lax.broadcasted_iota(jnp.int32, (batch, batch), 1)
+    load_labels.wait()
+    target = jnp.sum(jnp.where(row == col, labels[...].astype(F32), 0.0), axis=1, keepdims=True)
+    dlogit = 1.0 / (1.0 + jnp.exp(-logit)) - target
+
+    stores = []
+    size = grad_w.shape[1]
+    per_tower = CHUNKS // 2
+    dcomps = [(dlogit * slope).astype(BF16) for slope in slopes]
+    for i in range(CHUNKS):
+        k, part = i // per_tower, i % per_tower
+        grad_w[i] = contract_rows(feat[k, :, part * size : (part + 1) * size], dcomps[k])
+        store = pltpu.make_async_copy(
+            grad_w.at[i], grad_w_hbm.at[k, pl.ds(part * size, size)], sems.at[i]
+        )
+        store.start()
+        stores.append(store)
+    for k in range(2):
+        grad_x[k] = nt(dcomps[k], comp[k]).astype(BF16)
+
+    count = grad_down.shape[0]
+    first = (tower * lax.axis_size("member") + member) * count
+    own = lax.div(first, width)
+    offset = pl.multiple_of(lax.rem(first, width), count)
+    comp_f = compressed[own].astype(F32)
+    dgate_f = dlogit * wide[own] * comp_f
+    crossed = comp_f * gates[own] + comp_f
+    square[...] = contract_rows(dgate_f.astype(BF16), low)
+    grad_up[...] = square[pl.ds(offset, count), :]
+    square[...] = contract_rows(compressed[own], (dlogit * back).astype(BF16))
+    grad_down[...] = square[pl.ds(offset, count), :]
+    sums = jnp.concatenate(
+        [
+            jnp.sum(dgate_f, axis=0, keepdims=True),
+            jnp.sum(dlogit * crossed, axis=0, keepdims=True),
+            jnp.zeros((6, width), F32),
+        ],
+        axis=0,
+    )
+    vectors[...] = pltpu.roll(sums, width - offset, 1)[0:2, 0:count]
+    for store in stores:
+        store.wait()
+
+
+def shards_doubling(features, compress, top_down, top_up, top_bias, out_weight, labels):
+    local_towers, feat_rows, batch = features.shape
+    width = compress.shape[2]
+    rank = top_down.shape[1]
+    members = lax.axis_size("member")
+    top = top_down.shape[0]
+    count = top // (2 * members)
+    pieces = top // width
+    feat_t = jnp.swapaxes(features, 1, 2)
+    total = term(0, feat_t, compress) + exchange(term(1, feat_t, compress), 0, 1)
+    strides = [1 << bit for bit in range(1, members.bit_length() - 1)]
+    if len(strides) > 1:
+        one, two = strides.pop(0), strides.pop(0)
+        total = total + sum(exchange(total, 0, bits) for bits in (one, two, one | two))
+    for stride in strides:
+        total = total + exchange(total, 0, stride)
+    mine = total.astype(BF16)
+    near = lambda value: pltpu.with_memory_space_constraint(value, pltpu.VMEM)
+    grad_w, grad_x, grad_down, grad_up, vectors = pl.pallas_call(
+        top_kernel,
+        out_shape=(
+            jax.ShapeDtypeStruct((local_towers, feat_rows, width), F32),
+            jax.ShapeDtypeStruct((local_towers, batch, feat_rows), BF16),
+            jax.ShapeDtypeStruct((count, rank), F32),
+            jax.ShapeDtypeStruct((count, rank), F32),
+            jax.ShapeDtypeStruct((2, count), F32),
+        ),
+        in_specs=[VMEM] * 8 + [ANY, VMEM, VMEM],
+        out_specs=(ANY, VMEM, VMEM, VMEM, VMEM),
+        scratch_shapes=[
+            pltpu.VMEM((pieces, batch, width), BF16),
+            pltpu.VMEM((pieces, batch, width), F32),
+            pltpu.VMEM((pieces, 1, width), F32),
+            pltpu.VMEM((1, batch), labels.dtype),
+            pltpu.VMEM((CHUNKS, local_towers * feat_rows // CHUNKS, width), F32),
+            pltpu.VMEM((width, rank), F32),
+            pltpu.SemaphoreType.DMA((CHUNKS + 1,)),
+        ],
+        compiler_params=pltpu.CompilerParams(vmem_limit_bytes=8 << 20),
+        cost_estimate=pl.CostEstimate(
+            flops=10 * batch * top * rank, bytes_accessed=4 << 20, transcendentals=batch
+        ),
+    )(
+        near(mine),
+        near(exchange(mine, 0, 1)),
+        near(exchange(mine, 1, 0)),
+        near(exchange(mine, 1, 1)),
+        near(top_down),
+        near(top_up),
+        near(top_bias.reshape(1, top)),
+        near(out_weight.reshape(1, top)),
+        pltpu.with_memory_space_constraint(labels.reshape(1, batch), pltpu.HBM),
+        near(feat_t),
+        near(compress),
+    )
+    return grad_w, jnp.swapaxes(grad_x, 1, 2), grad_down, grad_up, vectors
+
+
+def shards(features, compress, top_down, *rest):
+    towers, members = lax.axis_size("tower"), lax.axis_size("member")
+    small = towers == 2 and features.shape[0] == 2 and features.shape[2] <= 128
+    power = members > 1 and members & (members - 1) == 0
+    body = shards_doubling if small and power else shards_spread
+    return body(features, compress, top_down, *rest)
+
+
 def solution(mesh):
     placed = (P("tower", "member", None), P("tower", "member", None), P(), P(), P(), P(), P())
     return jax.shard_map(

time: 265 us -> 24.5 us (0.09)
  waiting for transfers between devices: 142 us -> 8.85 us
  blocking collectives: 96.1 us -> 0 us
  between operations: 14.5 us -> 0.75 us
  starting transfers between devices: 0.12 us -> 9.36 us
  local copies, waits for them, and re-layouts: 5.76 us -> 0.04 us
  matrix products: 5.49 us -> 0 us
  Pallas kernels: 0 us -> 5.27 us
    reduce_scatter x2 -> x0, waiting for transfers between devices: 117 us -> none  [the longest x1 59.3 us: shards(): lax.psum_scatter(grad_down, 'member', scatter_dimension=0, tiled=True)]
    unnamed x1 -> x0, blocking collectives: 63.9 us -> none
    unnamed x4 -> x0, waiting for transfers between devices: 25.1 us -> none
    all_gather x1 -> x0, blocking collectives: 17.4 us -> none  [shards(): piece = lax.all_gather(dcomp, 'member', axis=0, tiled=True)]
    psum x3 -> x0, blocking collectives: 14.8 us -> none  [shards(): lax.psum(value, 'tower')]
    ppermute x0 -> x8, starting transfers between devices: none -> 9.36 us  [exchange(): return lax.ppermute(value, ('tower', 'member'), pairs)]
    ppermute x0 -> x8, waiting for transfers between devices: none -> 8.85 us  [exchange(): return lax.ppermute(value, ('tower', 'member'), pairs)]
    unnamed x20 -> x12, local copies, waits for them, and re-layouts: 5.64 us -> 0.03 us
  transfers between devices with their start and end apart: 3 -> 8, of which waited for: 3 -> 6; matrix products, arithmetic and copies ran while one was open for 2% -> 0% of each run, Pallas kernels for 0% -> 5%
where the time goes in v2:
time: 24.5 us; the launch traced here: 24.3 us
  starting transfers between devices  9.36 us (38%)
  waiting for transfers between devices  8.85 us (36%)
  Pallas kernels  5.27 us (22%)
  between operations  0.75 us (3%)
    ppermute x8, starting transfers between devices, exchange(): return lax.ppermute(value, ('tower', 'member'), pairs)  9.36 us
    ppermute x8, waiting for transfers between devices, exchange(): return lax.ppermute(value, ('tower', 'member'), pairs)  8.85 us
    pallas_call x1, Pallas kernels, shards_doubling(): pl.pallas_call(top_kernel, out_shape=(jax.ShapeDtypeStruct((local_towers,...  2.75 us
    pallas_call x2, Pallas kernels, term(): pl.pallas_call(lambda *refs: term_kernel(flip, *refs), out_shape=jax.Shap...  2.52 us
  transfers between devices with their start and end apart: 8, of which 6 were waited for; matrix products, arithmetic and copies ran while one was open for 0% of the time, Pallas kernels for 5%

profile of v2, /device:TPU:0, one launch (start us, length us, event | category | flops | bytes accessed | tf_op | source)
XLA Modules:
  0.0 24.3 jit_solution(10004273469015780630)
XLA Ops:
  0.6 0.0 copy-start.3
  0.6 1.3 %shard_map.111 = f32[64,256]{1,0:T(8,128)S(1)} custom-call(bf16[2,64,512]{2,1,0:T(8,128)(2,1)} %bitcast.4, bf16[2,512,256]{2,1,0:T(8,128)(2,1)} %comp.1), custom_call_target="tpu_custom_call" | custom-call | flops 16777216 | bytes 327680 | tf_op jit(solution)/shard_map/pallas_call | solution.py:140
  1.9 0.5 %collective-permute-start = (f32[64,256]{1,0:T(8,128)S(1)}, f32[64,256]{1,0:T(8,128)S(1)}, u32[]{:S(2)}, u32[]{:S(2)}) collective-permute-start(f32[64,256]{1,0:T(8,128)S(1)} %shard_map.111), channel_id=1, source_target_pairs={{0,1},{1,0},{2,3},{3,2},{4,5},{5,4},{6,7},{7,6},{8,9},{9,8},{10,11... | collective-permute-start | bytes 196616 | tf_op jit(solution)/shard_map/ppermute | solution.py:112
  2.4 0.0 copy-start.2
  2.4 1.3 %shard_map.110 = f32[64,256]{1,0:T(8,128)S(1)} custom-call(bf16[2,64,512]{2,1,0:T(8,128)(2,1)} %bitcast.5, bf16[2,512,256]{2,1,0:T(8,128)(2,1)} %comp.1), custom_call_target="tpu_custom_call" | custom-call | flops 16777216 | bytes 327680 | tf_op jit(solution)/shard_map/pallas_call | solution.py:140
  3.7 0.0 copy-start
  3.7 0.0 collective-permute-done
  3.7 3.6 %collective-permute-start.3 = (f32[64,256]{1,0:T(8,128)S(1)}, f32[64,256]{1,0:T(8,128)S(1)}, u32[]{:S(2)}, u32[]{:S(2)}) collective-permute-start(f32[64,256]{1,0:T(8,128)S(1)} %add.15), channel_id=1, source_target_pairs={{0,6},{1,7},{2,4},{3,5},{4,2},{5,3},{6,0},{7,1},{8,14},{9,15},{10,... | collective-permute-start | bytes 196616 | tf_op jit(solution)/shard_map/ppermute | solution.py:112
  7.4 0.4 %collective-permute-start.2 = (f32[64,256]{1,0:T(8,128)S(1)}, f32[64,256]{1,0:T(8,128)S(1)}, u32[]{:S(2)}, u32[]{:S(2)}) collective-permute-start(f32[64,256]{1,0:T(8,128)S(1)} %add.15), channel_id=1, source_target_pairs={{0,4},{1,5},{2,6},{3,7},{4,0},{5,1},{6,2},{7,3},{8,12},{9,13},{10,... | collective-permute-start | bytes 196616 | tf_op jit(solution)/shard_map/ppermute | solution.py:112
  7.8 0.2 collective-permute-start.1
  8.0 2.1 %collective-permute-done.3 = f32[64,256]{1,0:T(8,128)S(1)} collective-permute-done((f32[64,256]{1,0:T(8,128)S(1)}, f32[64,256]{1,0:T(8,128)S(1)}, u32[]{:S(2)}, u32[]{:S(2)}) %collective-permute-start.3) | collective-permute-done | bytes 65568 | tf_op jit(solution)/shard_map/ppermute | solution.py:112
  10.1 1.6 %collective-permute-done.2 = f32[64,256]{1,0:T(8,128)S(1)} collective-permute-done((f32[64,256]{1,0:T(8,128)S(1)}, f32[64,256]{1,0:T(8,128)S(1)}, u32[]{:S(2)}, u32[]{:S(2)}) %collective-permute-start.2) | collective-permute-done | bytes 65568 | tf_op jit(solution)/shard_map/ppermute | solution.py:112
  11.7 0.4 %collective-permute-done.1 = f32[64,256]{1,0:T(8,128)S(1)} collective-permute-done((f32[64,256]{1,0:T(8,128)S(1)}, f32[64,256]{1,0:T(8,128)S(1)}, u32[]{:S(2)}, u32[]{:S(2)}) %collective-permute-start.1) | collective-permute-done | bytes 65568 | tf_op jit(solution)/shard_map/ppermute | solution.py:112
  12.1 0.0 copy-start.5
  12.1 0.0 copy-start.1
  12.1 2.7 %collective-permute-start.4 = (f32[64,256]{1,0:T(8,128)S(1)}, f32[64,256]{1,0:T(8,128)S(1)}, u32[]{:S(2)}, u32[]{:S(2)}) collective-permute-start(f32[64,256]{1,0:T(8,128)S(1)} %add_add_fusion), channel_id=1, source_target_pairs={{0,8},{1,9},{2,10},{3,11},{4,12},{5,13},{6,14},{7,15},{8,0},{9,1},... | collective-permute-start | bytes 196616 | tf_op jit(solution)/shard_map/ppermute | solution.py:112
  14.8 2.6 %collective-permute-done.4 = f32[64,256]{1,0:T(8,128)S(1)} collective-permute-done((f32[64,256]{1,0:T(8,128)S(1)}, f32[64,256]{1,0:T(8,128)S(1)}, u32[]{:S(2)}, u32[]{:S(2)}) %collective-permute-start.4) | collective-permute-done | bytes 65568 | tf_op jit(solution)/shard_map/ppermute | solution.py:112
  17.4 0.0 copy-start.4
  17.4 0.1 collective-permute-start.7
  17.5 1.6 %collective-permute-start.6 = (bf16[64,256]{1,0:T(8,128)(2,1)S(1)}, bf16[64,256]{1,0:T(8,128)(2,1)S(1)}, u32[]{:S(2)}, u32[]{:S(2)}) collective-permute-start(bf16[64,256]{1,0:T(8,128)(2,1)S(1)} %add_convert_fusion.mine), channel_id=1, source_target_pairs={{0,16},{1,17},{2,18},{3,19},{4,20},{5,21},{6,22},{7,23},{8,24},{9,... | collective-permute-start | bytes 98312 | tf_op jit(solution)/shard_map/ppermute | solution.py:112
  19.0 0.3 %collective-permute-start.5 = (bf16[64,256]{1,0:T(8,128)(2,1)S(1)}, bf16[64,256]{1,0:T(8,128)(2,1)S(1)}, u32[]{:S(2)}, u32[]{:S(2)}) collective-permute-start(bf16[64,256]{1,0:T(8,128)(2,1)S(1)} %add_convert_fusion.mine), channel_id=1, source_target_pairs={{0,1},{1,0},{2,3},{3,2},{4,5},{5,4},{6,7},{7,6},{8,9},{9,8},{10,11... | collective-permute-start | bytes 98312 | tf_op jit(solution)/shard_map/ppermute | solution.py:112
  19.3 0.0 copy-done.5
  19.3 1.8 %collective-permute-done.7.both_piece = bf16[64,256]{1,0:T(8,128)(2,1)S(1)} collective-permute-done((bf16[64,256]{1,0:T(8,128)(2,1)S(1)}, bf16[64,256]{1,0:T(8,128)(2,1)S(1)}, u32[]{:S(2)}, u32[]{:S(2)}) %collective-permute-start.7) | collective-permute-done | bytes 32800 | tf_op jit(solution)/shard_map/ppermute | solution.py:112
  21.1 0.4 %collective-permute-done.6.tower_piece = bf16[64,256]{1,0:T(8,128)(2,1)S(1)} collective-permute-done((bf16[64,256]{1,0:T(8,128)(2,1)S(1)}, bf16[64,256]{1,0:T(8,128)(2,1)S(1)}, u32[]{:S(2)}, u32[]{:S(2)}) %collective-permute-start.6) | collective-permute-done | bytes 32800 | tf_op jit(solution)/shard_map/ppermute | solution.py:112
  21.5 0.0 collective-permute-done.5.side_piece
  21.5 0.0 copy-done.3
  21.5 0.0 copy-done.2
  21.5 0.0 copy-done
  21.5 0.0 copy-done.1
  21.5 0.0 copy-done.4
  21.6 2.8 %shard_map.112 = (f32[2,512,256]{2,1,0:T(8,128)}, bf16[2,64,512]{2,1,0:T(8,128)(2,1)}, f32[32,256]{1,0:T(8,128)}, f32[32,256]{1,0:T(8,128)}, f32[2,32]{1,0:T(2,128)}) custom-call(bf16[64,256]{1,0:T(8,128)(2,1)S(1)} %add_convert_fusion.mine, bf16[64,256]{1,0:T(8,128)(2,1)S(1)} %collective-permute-done.5.side_piece, ...), custom_call_target="tpu_custom_call" | custom-call | flops 167772160 | bytes 4194304 | tf_op jit(solution)/shard_map/pallas_call | solution.py:265
  (4 shorter events, 0.0 us)
Async XLA Ops:
  0.6 20.9 %copy-start.3 = (bf16[1024,256]{1,0:T(8,128)(2,1)S(1)}, bf16[1024,256]{1,0:T(8,128)(2,1)}, u32[]{:S(2)}) copy-start(bf16[1024,256]{1,0:T(8,128)(2,1)} %upper.1) | copy-start | bytes 1572868
  1.9 1.8 %collective-permute-start = (f32[64,256]{1,0:T(8,128)S(1)}, f32[64,256]{1,0:T(8,128)S(1)}, u32[]{:S(2)}, u32[]{:S(2)}) collective-permute-start(f32[64,256]{1,0:T(8,128)S(1)} %shard_map.111), channel_id=1, source_target_pairs={{0,1},{1,0},{2,3},{3,2},{4,5},{5,4},{6,7},{7,6},{8,9},{9,8},{10,11... | collective-permute-start | bytes 196616 | tf_op jit(solution)/shard_map/ppermute | solution.py:112
  2.4 19.1 %copy-start.2 = (bf16[1024,256]{1,0:T(8,128)(2,1)S(1)}, bf16[1024,256]{1,0:T(8,128)(2,1)}, u32[]{:S(2)}) copy-start(bf16[1024,256]{1,0:T(8,128)(2,1)} %down.1) | copy-start | bytes 1572868
  3.7 17.8 %copy-start = (bf16[2,512,256]{2,1,0:T(8,128)(2,1)S(1)}, bf16[2,512,256]{2,1,0:T(8,128)(2,1)}, u32[]{:S(2)}) copy-start(bf16[2,512,256]{2,1,0:T(8,128)(2,1)} %comp.1) | copy-start | bytes 1572868
  3.7 6.4 %collective-permute-start.3 = (f32[64,256]{1,0:T(8,128)S(1)}, f32[64,256]{1,0:T(8,128)S(1)}, u32[]{:S(2)}, u32[]{:S(2)}) collective-permute-start(f32[64,256]{1,0:T(8,128)S(1)} %add.15), channel_id=1, source_target_pairs={{0,6},{1,7},{2,4},{3,5},{4,2},{5,3},{6,0},{7,1},{8,14},{9,15},{10,... | collective-permute-start | bytes 196616 | tf_op jit(solution)/shard_map/ppermute | solution.py:112
  7.4 4.3 %collective-permute-start.2 = (f32[64,256]{1,0:T(8,128)S(1)}, f32[64,256]{1,0:T(8,128)S(1)}, u32[]{:S(2)}, u32[]{:S(2)}) collective-permute-start(f32[64,256]{1,0:T(8,128)S(1)} %add.15), channel_id=1, source_target_pairs={{0,4},{1,5},{2,6},{3,7},{4,0},{5,1},{6,2},{7,3},{8,12},{9,13},{10,... | collective-permute-start | bytes 196616 | tf_op jit(solution)/shard_map/ppermute | solution.py:112
  7.8 4.3 %collective-permute-start.1 = (f32[64,256]{1,0:T(8,128)S(1)}, f32[64,256]{1,0:T(8,128)S(1)}, u32[]{:S(2)}, u32[]{:S(2)}) collective-permute-start(f32[64,256]{1,0:T(8,128)S(1)} %add.15), channel_id=1, source_target_pairs={{0,2},{1,3},{2,0},{3,1},{4,6},{5,7},{6,4},{7,5},{8,10},{9,11},{10,... | collective-permute-start | bytes 196616 | tf_op jit(solution)/shard_map/ppermute | solution.py:112
  12.1 7.2 %copy-start.5 = (bf16[1024]{0:T(1024)(128)(2,1)S(1)}, bf16[1024]{0:T(1024)(128)(2,1)}, u32[]{:S(2)}) copy-start(bf16[1024]{0:T(1024)(128)(2,1)} %param.12) | copy-start | bytes 6148
  12.1 9.4 %copy-start.1 = (bf16[2,512,64]{1,2,0:T(8,128)(2,1)S(1)}, bf16[2,512,64]{1,2,0:T(8,128)(2,1)}, u32[]{:S(2)}) copy-start(bf16[2,512,64]{1,2,0:T(8,128)(2,1)} %param.7) | copy-start | bytes 393220
  12.1 5.3 %collective-permute-start.4 = (f32[64,256]{1,0:T(8,128)S(1)}, f32[64,256]{1,0:T(8,128)S(1)}, u32[]{:S(2)}, u32[]{:S(2)}) collective-permute-start(f32[64,256]{1,0:T(8,128)S(1)} %add_add_fusion), channel_id=1, source_target_pairs={{0,8},{1,9},{2,10},{3,11},{4,12},{5,13},{6,14},{7,15},{8,0},{9,1},... | collective-permute-start | bytes 196616 | tf_op jit(solution)/shard_map/ppermute | solution.py:112
  17.4 4.2 %copy-start.4 = (f32[1024]{0:T(1024)S(1)}, f32[1024]{0:T(1024)}, u32[]{:S(2)}) copy-start(f32[1024]{0:T(1024)} %param.11) | copy-start | bytes 12292
  17.4 3.7 %collective-permute-start.7 = (bf16[64,256]{1,0:T(8,128)(2,1)S(1)}, bf16[64,256]{1,0:T(8,128)(2,1)S(1)}, u32[]{:S(2)}, u32[]{:S(2)}) collective-permute-start(bf16[64,256]{1,0:T(8,128)(2,1)S(1)} %add_convert_fusion.mine), channel_id=1, source_target_pairs={{0,17},{1,16},{2,19},{3,18},{4,21},{5,20},{6,23},{7,22},{8,25},{9,... | collective-permute-start | bytes 98312 | tf_op jit(solution)/shard_map/ppermute | solution.py:112
  17.5 4.0 %collective-permute-start.6 = (bf16[64,256]{1,0:T(8,128)(2,1)S(1)}, bf16[64,256]{1,0:T(8,128)(2,1)S(1)}, u32[]{:S(2)}, u32[]{:S(2)}) collective-permute-start(bf16[64,256]{1,0:T(8,128)(2,1)S(1)} %add_convert_fusion.mine), channel_id=1, source_target_pairs={{0,16},{1,17},{2,18},{3,19},{4,20},{5,21},{6,22},{7,23},{8,24},{9,... | collective-permute-start | bytes 98312 | tf_op jit(solution)/shard_map/ppermute | solution.py:112
  19.0 2.5 %collective-permute-start.5 = (bf16[64,256]{1,0:T(8,128)(2,1)S(1)}, bf16[64,256]{1,0:T(8,128)(2,1)S(1)}, u32[]{:S(2)}, u32[]{:S(2)}) collective-permute-start(bf16[64,256]{1,0:T(8,128)(2,1)S(1)} %add_convert_fusion.mine), channel_id=1, source_target_pairs={{0,1},{1,0},{2,3},{3,2},{4,5},{5,4},{6,7},{7,6},{8,9},{9,8},{10,11... | collective-permute-start | bytes 98312 | tf_op jit(solution)/shard_map/ppermute | solution.py:112

commit v3 on v2

--- a/solution.py
+++ b/solution.py
@@ -159,14 +159,14 @@
 
 def top_kernel(
     mine, side_piece, tower_piece, both_piece, down, upper, bias, wout, labels_hbm, feat, comp,
-    grad_w_hbm, grad_x, grad_down, grad_up, vectors,
-    compressed, gates, wide, labels, grad_w, square, sems,
+    grad_w_hbm, grad_x_hbm, grad_down_hbm, grad_up_hbm, vectors_hbm,
+    compressed, gates, wide, labels, grad_w, grad_x, up_square, down_square, vectors, sems,
 ):
     tower, member = lax.axis_index("tower"), lax.axis_index("member")
     side = lax.rem(member, 2)
     batch, width = mine.shape
     pieces = compressed.shape[0]
-    load_labels = pltpu.make_async_copy(labels_hbm, labels, sems.at[CHUNKS])
+    load_labels = pltpu.make_async_copy(labels_hbm, labels, sems.at[CHUNKS + 5])
     load_labels.start()
     compressed[2 * tower + side] = mine[...]
     compressed[2 * tower + 1 - side] = side_piece[...]
@@ -206,31 +206,33 @@
     dlogit = 1.0 / (1.0 + jnp.exp(-logit)) - target
 
     stores = []
+
+    def send(source, target):
+        stores.append(pltpu.make_async_copy(source, target, sems.at[len(stores)]))
+        stores[-1].start()
+
     size = grad_w.shape[1]
     per_tower = CHUNKS // 2
     dcomps = [(dlogit * slope).astype(BF16) for slope in slopes]
     for i in range(CHUNKS):
         k, part = i // per_tower, i % per_tower
         grad_w[i] = contract_rows(feat[k, :, part * size : (part + 1) * size], dcomps[k])
-        store = pltpu.make_async_copy(
-            grad_w.at[i], grad_w_hbm.at[k, pl.ds(part * size, size)], sems.at[i]
-        )
-        store.start()
-        stores.append(store)
+        send(grad_w.at[i], grad_w_hbm.at[k, pl.ds(part * size, size)])
     for k in range(2):
         grad_x[k] = nt(dcomps[k], comp[k]).astype(BF16)
-
-    count = grad_down.shape[0]
+        send(grad_x.at[k], grad_x_hbm.at[k])
+
+    count = grad_down_hbm.shape[0]
     first = (tower * lax.axis_size("member") + member) * count
     own = lax.div(first, width)
     offset = pl.multiple_of(lax.rem(first, width), count)
     comp_f = compressed[own].astype(F32)
     dgate_f = dlogit * wide[own] * comp_f
     crossed = comp_f * gates[own] + comp_f
-    square[...] = contract_rows(dgate_f.astype(BF16), low)
-    grad_up[...] = square[pl.ds(offset, count), :]
-    square[...] = contract_rows(compressed[own], (dlogit * back).astype(BF16))
-    grad_down[...] = square[pl.ds(offset, count), :]
+    up_square[...] = contract_rows(dgate_f.astype(BF16), low)
+    send(up_square.at[pl.ds(offset, count)], grad_up_hbm)
+    down_square[...] = contract_rows(compressed[own], (dlogit * back).astype(BF16))
+    send(down_square.at[pl.ds(offset, count)], grad_down_hbm)
     sums = jnp.concatenate(
         [
             jnp.sum(dgate_f, axis=0, keepdims=True),
@@ -240,6 +242,7 @@
         axis=0,
     )
     vectors[...] = pltpu.roll(sums, width - offset, 1)[0:2, 0:count]
+    send(vectors, vectors_hbm)
     for store in stores:
         store.wait()
 
@@ -272,15 +275,18 @@
             jax.ShapeDtypeStruct((2, count), F32),
         ),
         in_specs=[VMEM] * 8 + [ANY, VMEM, VMEM],
-        out_specs=(ANY, VMEM, VMEM, VMEM, VMEM),
+        out_specs=(ANY,) * 5,
         scratch_shapes=[
             pltpu.VMEM((pieces, batch, width), BF16),
             pltpu.VMEM((pieces, batch, width), F32),
             pltpu.VMEM((pieces, 1, width), F32),
             pltpu.VMEM((1, batch), labels.dtype),
             pltpu.VMEM((CHUNKS, local_towers * feat_rows // CHUNKS, width), F32),
+            pltpu.VMEM((local_towers, batch, feat_rows), BF16),
             pltpu.VMEM((width, rank), F32),
-            pltpu.SemaphoreType.DMA((CHUNKS + 1,)),
+            pltpu.VMEM((width, rank), F32),
+            pltpu.VMEM((2, count), F32),
+            pltpu.SemaphoreType.DMA((CHUNKS + 6,)),
         ],
         compiler_params=pltpu.CompilerParams(vmem_limit_bytes=8 << 20),
         cost_estimate=pl.CostEstimate(

time: 24.5 us -> 23.9 us (0.976)
  Pallas kernels: 5.27 us -> 4.67 us
    pallas_call x1, Pallas kernels: 2.75 us -> 2.15 us  [shards_doubling(): pl.pallas_call(top_kernel, out_shape=(jax.ShapeDtypeStruct((local_towers,...]
where the time goes in v3:
time: 23.9 us; the launch traced here: 23.7 us
  starting transfers between devices  9.36 us (39%)
  waiting for transfers between devices  8.85 us (37%)
  Pallas kernels  4.67 us (20%)
  between operations  0.75 us (3%)
    ppermute x8, starting transfers between devices, exchange(): return lax.ppermute(value, ('tower', 'member'), pairs)  9.36 us
    ppermute x8, waiting for transfers between devices, exchange(): return lax.ppermute(value, ('tower', 'member'), pairs)  8.85 us
    pallas_call x2, Pallas kernels, term(): pl.pallas_call(lambda *refs: term_kernel(flip, *refs), out_shape=jax.Shap...  2.52 us
    pallas_call x1, Pallas kernels, shards_doubling(): pl.pallas_call(top_kernel, out_shape=(jax.ShapeDtypeStruct((local_towers,...  2.15 us
  transfers between devices with their start and end apart: 8, of which 6 were waited for; matrix products, arithmetic and copies ran while one was open for 0% of the time, Pallas kernels for 5%

profile of v3, /device:TPU:0, one launch (start us, length us, event | category | flops | bytes accessed | tf_op | source)
XLA Modules:
  0.0 23.7 jit_solution(13985769099092712125)
XLA Ops:
  0.6 0.0 copy-start.3
  0.6 1.3 %shard_map.111 = f32[64,256]{1,0:T(8,128)S(1)} custom-call(bf16[2,64,512]{2,1,0:T(8,128)(2,1)} %bitcast.4, bf16[2,512,256]{2,1,0:T(8,128)(2,1)} %comp.1), custom_call_target="tpu_custom_call" | custom-call | flops 16777216 | bytes 327680 | tf_op jit(solution)/shard_map/pallas_call | solution.py:140
  1.9 0.5 %collective-permute-start = (f32[64,256]{1,0:T(8,128)S(1)}, f32[64,256]{1,0:T(8,128)S(1)}, u32[]{:S(2)}, u32[]{:S(2)}) collective-permute-start(f32[64,256]{1,0:T(8,128)S(1)} %shard_map.111), channel_id=1, source_target_pairs={{0,1},{1,0},{2,3},{3,2},{4,5},{5,4},{6,7},{7,6},{8,9},{9,8},{10,11... | collective-permute-start | bytes 196616 | tf_op jit(solution)/shard_map/ppermute | solution.py:112
  2.4 0.0 copy-start.2
  2.4 1.3 %shard_map.110 = f32[64,256]{1,0:T(8,128)S(1)} custom-call(bf16[2,64,512]{2,1,0:T(8,128)(2,1)} %bitcast.5, bf16[2,512,256]{2,1,0:T(8,128)(2,1)} %comp.1), custom_call_target="tpu_custom_call" | custom-call | flops 16777216 | bytes 327680 | tf_op jit(solution)/shard_map/pallas_call | solution.py:140
  3.7 0.0 copy-start
  3.7 0.0 collective-permute-done
  3.7 3.6 %collective-permute-start.3 = (f32[64,256]{1,0:T(8,128)S(1)}, f32[64,256]{1,0:T(8,128)S(1)}, u32[]{:S(2)}, u32[]{:S(2)}) collective-permute-start(f32[64,256]{1,0:T(8,128)S(1)} %add.15), channel_id=1, source_target_pairs={{0,6},{1,7},{2,4},{3,5},{4,2},{5,3},{6,0},{7,1},{8,14},{9,15},{10,... | collective-permute-start | bytes 196616 | tf_op jit(solution)/shard_map/ppermute | solution.py:112
  7.4 0.4 %collective-permute-start.2 = (f32[64,256]{1,0:T(8,128)S(1)}, f32[64,256]{1,0:T(8,128)S(1)}, u32[]{:S(2)}, u32[]{:S(2)}) collective-permute-start(f32[64,256]{1,0:T(8,128)S(1)} %add.15), channel_id=1, source_target_pairs={{0,4},{1,5},{2,6},{3,7},{4,0},{5,1},{6,2},{7,3},{8,12},{9,13},{10,... | collective-permute-start | bytes 196616 | tf_op jit(solution)/shard_map/ppermute | solution.py:112
  7.8 0.2 collective-permute-start.1
  8.0 2.1 %collective-permute-done.3 = f32[64,256]{1,0:T(8,128)S(1)} collective-permute-done((f32[64,256]{1,0:T(8,128)S(1)}, f32[64,256]{1,0:T(8,128)S(1)}, u32[]{:S(2)}, u32[]{:S(2)}) %collective-permute-start.3) | collective-permute-done | bytes 65568 | tf_op jit(solution)/shard_map/ppermute | solution.py:112
  10.1 1.6 %collective-permute-done.2 = f32[64,256]{1,0:T(8,128)S(1)} collective-permute-done((f32[64,256]{1,0:T(8,128)S(1)}, f32[64,256]{1,0:T(8,128)S(1)}, u32[]{:S(2)}, u32[]{:S(2)}) %collective-permute-start.2) | collective-permute-done | bytes 65568 | tf_op jit(solution)/shard_map/ppermute | solution.py:112
  11.7 0.4 %collective-permute-done.1 = f32[64,256]{1,0:T(8,128)S(1)} collective-permute-done((f32[64,256]{1,0:T(8,128)S(1)}, f32[64,256]{1,0:T(8,128)S(1)}, u32[]{:S(2)}, u32[]{:S(2)}) %collective-permute-start.1) | collective-permute-done | bytes 65568 | tf_op jit(solution)/shard_map/ppermute | solution.py:112
  12.1 0.0 copy-start.5
  12.1 0.0 copy-start.1
  12.1 2.7 %collective-permute-start.4 = (f32[64,256]{1,0:T(8,128)S(1)}, f32[64,256]{1,0:T(8,128)S(1)}, u32[]{:S(2)}, u32[]{:S(2)}) collective-permute-start(f32[64,256]{1,0:T(8,128)S(1)} %add_add_fusion), channel_id=1, source_target_pairs={{0,8},{1,9},{2,10},{3,11},{4,12},{5,13},{6,14},{7,15},{8,0},{9,1},... | collective-permute-start | bytes 196616 | tf_op jit(solution)/shard_map/ppermute | solution.py:112
  14.8 2.6 %collective-permute-done.4 = f32[64,256]{1,0:T(8,128)S(1)} collective-permute-done((f32[64,256]{1,0:T(8,128)S(1)}, f32[64,256]{1,0:T(8,128)S(1)}, u32[]{:S(2)}, u32[]{:S(2)}) %collective-permute-start.4) | collective-permute-done | bytes 65568 | tf_op jit(solution)/shard_map/ppermute | solution.py:112
  17.4 0.0 copy-start.4
  17.4 0.1 collective-permute-start.7
  17.5 1.6 %collective-permute-start.6 = (bf16[64,256]{1,0:T(8,128)(2,1)S(1)}, bf16[64,256]{1,0:T(8,128)(2,1)S(1)}, u32[]{:S(2)}, u32[]{:S(2)}) collective-permute-start(bf16[64,256]{1,0:T(8,128)(2,1)S(1)} %add_convert_fusion.mine), channel_id=1, source_target_pairs={{0,16},{1,17},{2,18},{3,19},{4,20},{5,21},{6,22},{7,23},{8,24},{9,... | collective-permute-start | bytes 98312 | tf_op jit(solution)/shard_map/ppermute | solution.py:112
  19.0 0.3 %collective-permute-start.5 = (bf16[64,256]{1,0:T(8,128)(2,1)S(1)}, bf16[64,256]{1,0:T(8,128)(2,1)S(1)}, u32[]{:S(2)}, u32[]{:S(2)}) collective-permute-start(bf16[64,256]{1,0:T(8,128)(2,1)S(1)} %add_convert_fusion.mine), channel_id=1, source_target_pairs={{0,1},{1,0},{2,3},{3,2},{4,5},{5,4},{6,7},{7,6},{8,9},{9,8},{10,11... | collective-permute-start | bytes 98312 | tf_op jit(solution)/shard_map/ppermute | solution.py:112
  19.3 0.0 copy-done.5
  19.3 1.8 %collective-permute-done.7.both_piece = bf16[64,256]{1,0:T(8,128)(2,1)S(1)} collective-permute-done((bf16[64,256]{1,0:T(8,128)(2,1)S(1)}, bf16[64,256]{1,0:T(8,128)(2,1)S(1)}, u32[]{:S(2)}, u32[]{:S(2)}) %collective-permute-start.7) | collective-permute-done | bytes 32800 | tf_op jit(solution)/shard_map/ppermute | solution.py:112
  21.1 0.4 %collective-permute-done.6.tower_piece = bf16[64,256]{1,0:T(8,128)(2,1)S(1)} collective-permute-done((bf16[64,256]{1,0:T(8,128)(2,1)S(1)}, bf16[64,256]{1,0:T(8,128)(2,1)S(1)}, u32[]{:S(2)}, u32[]{:S(2)}) %collective-permute-start.6) | collective-permute-done | bytes 32800 | tf_op jit(solution)/shard_map/ppermute | solution.py:112
  21.5 0.0 collective-permute-done.5.side_piece
  21.5 0.0 copy-done.3
  21.5 0.0 copy-done.2
  21.5 0.0 copy-done
  21.5 0.0 copy-done.1
  21.5 0.0 copy-done.4
  21.6 2.1 %shard_map.112 = (f32[2,512,256]{2,1,0:T(8,128)}, bf16[2,64,512]{2,1,0:T(8,128)(2,1)}, f32[32,256]{1,0:T(8,128)}, f32[32,256]{1,0:T(8,128)}, f32[2,32]{1,0:T(2,128)}) custom-call(bf16[64,256]{1,0:T(8,128)(2,1)S(1)} %add_convert_fusion.mine, bf16[64,256]{1,0:T(8,128)(2,1)S(1)} %collective-permute-done.5.side_piece, ...), custom_call_target="tpu_custom_call" | custom-call | flops 167772160 | bytes 4194304 | tf_op jit(solution)/shard_map/pallas_call | solution.py:268
  (4 shorter events, 0.0 us)
Async XLA Ops:
  0.6 20.9 %copy-start.3 = (bf16[1024,256]{1,0:T(8,128)(2,1)S(1)}, bf16[1024,256]{1,0:T(8,128)(2,1)}, u32[]{:S(2)}) copy-start(bf16[1024,256]{1,0:T(8,128)(2,1)} %upper.1) | copy-start | bytes 1572868
  1.9 1.8 %collective-permute-start = (f32[64,256]{1,0:T(8,128)S(1)}, f32[64,256]{1,0:T(8,128)S(1)}, u32[]{:S(2)}, u32[]{:S(2)}) collective-permute-start(f32[64,256]{1,0:T(8,128)S(1)} %shard_map.111), channel_id=1, source_target_pairs={{0,1},{1,0},{2,3},{3,2},{4,5},{5,4},{6,7},{7,6},{8,9},{9,8},{10,11... | collective-permute-start | bytes 196616 | tf_op jit(solution)/shard_map/ppermute | solution.py:112
  2.4 19.1 %copy-start.2 = (bf16[1024,256]{1,0:T(8,128)(2,1)S(1)}, bf16[1024,256]{1,0:T(8,128)(2,1)}, u32[]{:S(2)}) copy-start(bf16[1024,256]{1,0:T(8,128)(2,1)} %down.1) | copy-start | bytes 1572868
  3.7 17.8 %copy-start = (bf16[2,512,256]{2,1,0:T(8,128)(2,1)S(1)}, bf16[2,512,256]{2,1,0:T(8,128)(2,1)}, u32[]{:S(2)}) copy-start(bf16[2,512,256]{2,1,0:T(8,128)(2,1)} %comp.1) | copy-start | bytes 1572868
  3.7 6.4 %collective-permute-start.3 = (f32[64,256]{1,0:T(8,128)S(1)}, f32[64,256]{1,0:T(8,128)S(1)}, u32[]{:S(2)}, u32[]{:S(2)}) collective-permute-start(f32[64,256]{1,0:T(8,128)S(1)} %add.15), channel_id=1, source_target_pairs={{0,6},{1,7},{2,4},{3,5},{4,2},{5,3},{6,0},{7,1},{8,14},{9,15},{10,... | collective-permute-start | bytes 196616 | tf_op jit(solution)/shard_map/ppermute | solution.py:112
  7.4 4.3 %collective-permute-start.2 = (f32[64,256]{1,0:T(8,128)S(1)}, f32[64,256]{1,0:T(8,128)S(1)}, u32[]{:S(2)}, u32[]{:S(2)}) collective-permute-start(f32[64,256]{1,0:T(8,128)S(1)} %add.15), channel_id=1, source_target_pairs={{0,4},{1,5},{2,6},{3,7},{4,0},{5,1},{6,2},{7,3},{8,12},{9,13},{10,... | collective-permute-start | bytes 196616 | tf_op jit(solution)/shard_map/ppermute | solution.py:112
  7.8 4.3 %collective-permute-start.1 = (f32[64,256]{1,0:T(8,128)S(1)}, f32[64,256]{1,0:T(8,128)S(1)}, u32[]{:S(2)}, u32[]{:S(2)}) collective-permute-start(f32[64,256]{1,0:T(8,128)S(1)} %add.15), channel_id=1, source_target_pairs={{0,2},{1,3},{2,0},{3,1},{4,6},{5,7},{6,4},{7,5},{8,10},{9,11},{10,... | collective-permute-start | bytes 196616 | tf_op jit(solution)/shard_map/ppermute | solution.py:112
  12.1 7.2 %copy-start.5 = (bf16[1024]{0:T(1024)(128)(2,1)S(1)}, bf16[1024]{0:T(1024)(128)(2,1)}, u32[]{:S(2)}) copy-start(bf16[1024]{0:T(1024)(128)(2,1)} %param.12) | copy-start | bytes 6148
  12.1 9.4 %copy-start.1 = (bf16[2,512,64]{1,2,0:T(8,128)(2,1)S(1)}, bf16[2,512,64]{1,2,0:T(8,128)(2,1)}, u32[]{:S(2)}) copy-start(bf16[2,512,64]{1,2,0:T(8,128)(2,1)} %param.7) | copy-start | bytes 393220
  12.1 5.3 %collective-permute-start.4 = (f32[64,256]{1,0:T(8,128)S(1)}, f32[64,256]{1,0:T(8,128)S(1)}, u32[]{:S(2)}, u32[]{:S(2)}) collective-permute-start(f32[64,256]{1,0:T(8,128)S(1)} %add_add_fusion), channel_id=1, source_target_pairs={{0,8},{1,9},{2,10},{3,11},{4,12},{5,13},{6,14},{7,15},{8,0},{9,1},... | collective-permute-start | bytes 196616 | tf_op jit(solution)/shard_map/ppermute | solution.py:112
  17.4 4.2 %copy-start.4 = (f32[1024]{0:T(1024)S(1)}, f32[1024]{0:T(1024)}, u32[]{:S(2)}) copy-start(f32[1024]{0:T(1024)} %param.11) | copy-start | bytes 12292
  17.4 3.7 %collective-permute-start.7 = (bf16[64,256]{1,0:T(8,128)(2,1)S(1)}, bf16[64,256]{1,0:T(8,128)(2,1)S(1)}, u32[]{:S(2)}, u32[]{:S(2)}) collective-permute-start(bf16[64,256]{1,0:T(8,128)(2,1)S(1)} %add_convert_fusion.mine), channel_id=1, source_target_pairs={{0,17},{1,16},{2,19},{3,18},{4,21},{5,20},{6,23},{7,22},{8,25},{9,... | collective-permute-start | bytes 98312 | tf_op jit(solution)/shard_map/ppermute | solution.py:112
  17.5 4.0 %collective-permute-start.6 = (bf16[64,256]{1,0:T(8,128)(2,1)S(1)}, bf16[64,256]{1,0:T(8,128)(2,1)S(1)}, u32[]{:S(2)}, u32[]{:S(2)}) collective-permute-start(bf16[64,256]{1,0:T(8,128)(2,1)S(1)} %add_convert_fusion.mine), channel_id=1, source_target_pairs={{0,16},{1,17},{2,18},{3,19},{4,20},{5,21},{6,22},{7,23},{8,24},{9,... | collective-permute-start | bytes 98312 | tf_op jit(solution)/shard_map/ppermute | solution.py:112
  19.0 2.5 %collective-permute-start.5 = (bf16[64,256]{1,0:T(8,128)(2,1)S(1)}, bf16[64,256]{1,0:T(8,128)(2,1)S(1)}, u32[]{:S(2)}, u32[]{:S(2)}) collective-permute-start(bf16[64,256]{1,0:T(8,128)(2,1)S(1)} %add_convert_fusion.mine), channel_id=1, source_target_pairs={{0,1},{1,0},{2,3},{3,2},{4,5},{5,4},{6,7},{7,6},{8,9},{9,8},{10,11... | collective-permute-start | bytes 98312 | tf_op jit(solution)/shard_map/ppermute | solution.py:112

commit v4 on v3

--- a/solution.py
+++ b/solution.py
@@ -102,6 +102,10 @@
     return lax.dot_general(left, right, (((1,), (1,)), ((), ())), preferred_element_type=F32)
 
 
+def side_of(member):
+    return lax.rem(member, 2)
+
+
 def exchange(value, tower_bit, member_bit):
     towers, members = lax.axis_size("tower"), lax.axis_size("member")
     pairs = [
@@ -112,62 +116,95 @@
     return lax.ppermute(value, ("tower", "member"), pairs)
 
 
-def term_kernel(flip, feat_hbm, comp_hbm, out, feat, comp, sems):
-    which = lax.rem(lax.axis_index("member") + flip, 2)
-    rows = comp.shape[1]
-    load_feat = pltpu.make_async_copy(feat_hbm.at[which], feat, sems.at[2])
+def sent_kernel(feat_hbm, comp_hbm, out, feat, comp, sems):
+    which = 1 - side_of(lax.axis_index("member"))
+    parts, rows, _ = comp.shape
+    load_feat = pltpu.make_async_copy(feat_hbm.at[which], feat, sems.at[parts])
     loads = [
         pltpu.make_async_copy(
             comp_hbm.at[which, pl.ds(i * rows, rows)], comp.at[i], sems.at[i]
         )
-        for i in range(2)
+        for i in range(parts)
     ]
     load_feat.start()
     for load in loads:
         load.start()
     load_feat.wait()
     total = None
-    for i in range(2):
+    for i in range(parts):
         loads[i].wait()
         part = jnp.dot(feat[:, i * rows : (i + 1) * rows], comp[i], preferred_element_type=F32)
         total = part if total is None else total + part
     out[...] = total
 
 
-def term(flip, feat_t, compress):
+def kept_kernel(feat, comp, labels_hbm, out, target, labels, sem):
+    which = side_of(lax.axis_index("member"))
+    batch = feat.shape[1]
+    load_labels = pltpu.make_async_copy(labels_hbm, labels, sem)
+    load_labels.start()
+    out[...] = jnp.dot(feat[which], comp[which], preferred_element_type=F32)
+    load_labels.wait()
+    row = lax.broadcasted_iota(jnp.int32, (batch, batch), 0)
+    col = lax.broadcasted_iota(jnp.int32, (batch, batch), 1)
+    target[...] = jnp.sum(
+        jnp.where(row == col, labels[...].astype(F32), 0.0), axis=1, keepdims=True
+    )
+
+
+def near(value):
+    return pltpu.with_memory_space_constraint(value, pltpu.VMEM)
+
+
+def far(value):
+    return pltpu.with_memory_space_constraint(value, pltpu.HBM)
+
+
+def terms(feat_t, compress, labels):
     _, batch, rows = feat_t.shape
     width = compress.shape[2]
-    return pl.pallas_call(
-        lambda *refs: term_kernel(flip, *refs),
+    parts = 2
+    cost = pl.CostEstimate(
+        flops=2 * batch * rows * width, bytes_accessed=2 * rows * (width + batch), transcendentals=0
+    )
+    limit = pltpu.CompilerParams(vmem_limit_bytes=2 << 20)
+    sent = pl.pallas_call(
+        sent_kernel,
         out_shape=jax.ShapeDtypeStruct((batch, width), F32),
         in_specs=[ANY, ANY],
         out_specs=VMEM,
         scratch_shapes=[
             pltpu.VMEM((batch, rows), BF16),
-            pltpu.VMEM((2, rows // 2, width), BF16),
-            pltpu.SemaphoreType.DMA((3,)),
+            pltpu.VMEM((parts, rows // parts, width), BF16),
+            pltpu.SemaphoreType.DMA((parts + 1,)),
         ],
-        compiler_params=pltpu.CompilerParams(vmem_limit_bytes=2 << 20),
-        cost_estimate=pl.CostEstimate(
-            flops=2 * batch * rows * width, bytes_accessed=2 * rows * (width + batch), transcendentals=0
+        compiler_params=limit,
+        cost_estimate=cost,
+    )(far(feat_t), far(compress))
+    kept, target = pl.pallas_call(
+        kept_kernel,
+        out_shape=(
+            jax.ShapeDtypeStruct((batch, width), F32),
+            jax.ShapeDtypeStruct((batch, 1), F32),
         ),
-    )(
-        pltpu.with_memory_space_constraint(feat_t, pltpu.HBM),
-        pltpu.with_memory_space_constraint(compress, pltpu.HBM),
-    )
+        in_specs=[VMEM, VMEM, ANY],
+        out_specs=(VMEM, VMEM),
+        scratch_shapes=[pltpu.VMEM((1, batch), labels.dtype), pltpu.SemaphoreType.DMA],
+        compiler_params=limit,
+        cost_estimate=cost,
+    )(near(feat_t), near(compress), far(labels.reshape(1, batch)))
+    return sent, kept, target
 
 
 def top_kernel(
-    mine, side_piece, tower_piece, both_piece, down, upper, bias, wout, labels_hbm, feat, comp,
+    mine, side_piece, tower_piece, both_piece, down, upper, bias, wout, target, feat, comp,
     grad_w_hbm, grad_x_hbm, grad_down_hbm, grad_up_hbm, vectors_hbm,
-    compressed, gates, wide, labels, grad_w, grad_x, up_square, down_square, vectors, sems,
+    compressed, gates, wide, grad_w, grad_x, up_square, down_square, vectors, sems,
 ):
     tower, member = lax.axis_index("tower"), lax.axis_index("member")
-    side = lax.rem(member, 2)
+    side = side_of(member)
     batch, width = mine.shape
     pieces = compressed.shape[0]
-    load_labels = pltpu.make_async_copy(labels_hbm, labels, sems.at[CHUNKS + 5])
-    load_labels.start()
     compressed[2 * tower + side] = mine[...]
     compressed[2 * tower + 1 - side] = side_piece[...]
     compressed[2 * (1 - tower) + side] = tower_piece[...]
@@ -179,31 +216,30 @@
         jnp.dot(compressed[j], down[block(j), :], preferred_element_type=F32)
         for j in range(pieces)
     ).astype(BF16)
-    weighted, scores = [], []
+    weighted = [
+        (compressed[j].astype(F32) * wout[:, block(j)].astype(F32)).astype(BF16)
+        for j in range(pieces)
+    ]
+    back = summed(
+        jnp.dot(weighted[j], upper[block(j), :], preferred_element_type=F32)
+        for j in range(pieces)
+    )
+    back_low = back.astype(BF16)
+    scores = []
     for j in range(pieces):
         gate = nt(low, upper[block(j), :]) + bias[:, block(j)]
         gates[j] = gate
         out_row = wout[:, block(j)].astype(F32)
         wide[j] = out_row
         comp_f = compressed[j].astype(F32)
-        weighted.append((comp_f * out_row).astype(BF16))
         scores.append((comp_f * gate + comp_f) * out_row)
     logit = jnp.sum(summed(scores), axis=1, keepdims=True)
-    back = summed(
-        jnp.dot(weighted[j], upper[block(j), :], preferred_element_type=F32)
-        for j in range(pieces)
-    )
-    back_low = back.astype(BF16)
     slopes = []
     for k in range(2):
         j = 2 * tower + k
         rows = pl.ds(pl.multiple_of(j * width, width), width)
         slopes.append(wide[j] * (gates[j] + 1.0) + nt(back_low, down[rows, :]))
-    row = lax.broadcasted_iota(jnp.int32, (batch, batch), 0)
-    col = lax.broadcasted_iota(jnp.int32, (batch, batch), 1)
-    load_labels.wait()
-    target = jnp.sum(jnp.where(row == col, labels[...].astype(F32), 0.0), axis=1, keepdims=True)
-    dlogit = 1.0 / (1.0 + jnp.exp(-logit)) - target
+    dlogit = 1.0 / (1.0 + jnp.exp(-logit)) - target[...]
 
     stores = []
 
@@ -256,7 +292,8 @@
     count = top // (2 * members)
     pieces = top // width
     feat_t = jnp.swapaxes(features, 1, 2)
-    total = term(0, feat_t, compress) + exchange(term(1, feat_t, compress), 0, 1)
+    sent, kept, target = terms(feat_t, compress, labels)
+    total = kept + exchange(sent, 0, 1)
     strides = [1 << bit for bit in range(1, members.bit_length() - 1)]
     if len(strides) > 1:
         one, two = strides.pop(0), strides.pop(0)
@@ -264,7 +301,6 @@
     for stride in strides:
         total = total + exchange(total, 0, stride)
     mine = total.astype(BF16)
-    near = lambda value: pltpu.with_memory_space_constraint(value, pltpu.VMEM)
     grad_w, grad_x, grad_down, grad_up, vectors = pl.pallas_call(
         top_kernel,
         out_shape=(
@@ -274,19 +310,18 @@
             jax.ShapeDtypeStruct((count, rank), F32),
             jax.ShapeDtypeStruct((2, count), F32),
         ),
-        in_specs=[VMEM] * 8 + [ANY, VMEM, VMEM],
+        in_specs=[VMEM] * 11,
         out_specs=(ANY,) * 5,
         scratch_shapes=[
             pltpu.VMEM((pieces, batch, width), BF16),
             pltpu.VMEM((pieces, batch, width), F32),
             pltpu.VMEM((pieces, 1, width), F32),
-            pltpu.VMEM((1, batch), labels.dtype),
             pltpu.VMEM((CHUNKS, local_towers * feat_rows // CHUNKS, width), F32),
             pltpu.VMEM((local_towers, batch, feat_rows), BF16),
             pltpu.VMEM((width, rank), F32),
             pltpu.VMEM((width, rank), F32),
             pltpu.VMEM((2, count), F32),
-            pltpu.SemaphoreType.DMA((CHUNKS + 6,)),
+            pltpu.SemaphoreType.DMA((CHUNKS + 5,)),
         ],
         compiler_params=pltpu.CompilerParams(vmem_limit_bytes=8 << 20),
         cost_estimate=pl.CostEstimate(
@@ -301,7 +336,7 @@
         near(top_up),
         near(top_bias.reshape(1, top)),
         near(out_weight.reshape(1, top)),
-        pltpu.with_memory_space_constraint(labels.reshape(1, batch), pltpu.HBM),
+        near(target),
         near(feat_t),
         near(compress),
     )

time: 23.9 us -> 23.6 us (0.987)
  Pallas kernels: 4.67 us -> 4.14 us
  starting transfers between devices: 9.36 us -> 9.68 us
    pallas_call x2, Pallas kernels: 2.52 us -> 2.13 us  [the longest x1 1.27 us: terms(): pl.pallas_call(sent_kernel, out_shape=jax.ShapeDtypeStruct((batch, width)...]
    ppermute x8, starting transfers between devices: 9.36 us -> 9.68 us  [exchange(): return lax.ppermute(value, ('tower', 'member'), pairs)]
  transfers between devices with their start and end apart: 8 -> 8, of which waited for: 6 -> 6; matrix products, arithmetic and copies ran while one was open for 0% -> 0% of each run, Pallas kernels for 5% -> 4%
where the time goes in v4:
time: 23.6 us; the launch traced here: 23.5 us
  starting transfers between devices  9.68 us (41%)
  waiting for transfers between devices  8.84 us (37%)
  Pallas kernels  4.14 us (18%)
  between operations  0.72 us (3%)
    ppermute x8, starting transfers between devices, exchange(): return lax.ppermute(value, ('tower', 'member'), pairs)  9.68 us
    ppermute x8, waiting for transfers between devices, exchange(): return lax.ppermute(value, ('tower', 'member'), pairs)  8.84 us
    pallas_call x1, Pallas kernels, shards_doubling(): pl.pallas_call(top_kernel, out_shape=(jax.ShapeDtypeStruct((local_towers,...  2.01 us
    pallas_call x1, Pallas kernels, terms(): pl.pallas_call(sent_kernel, out_shape=jax.ShapeDtypeStruct((batch, width)...  1.27 us
    pallas_call x1, Pallas kernels, terms(): pl.pallas_call(kept_kernel, out_shape=(jax.ShapeDtypeStruct((batch, width...  0.86 us
  transfers between devices with their start and end apart: 8, of which 6 were waited for; matrix products, arithmetic and copies ran while one was open for 0% of the time, Pallas kernels for 4%

profile of v4, /device:TPU:0, one launch (start us, length us, event | category | flops | bytes accessed | tf_op | source)
XLA Modules:
  0.0 23.5 jit_solution(14997439388923697359)
XLA Ops:
  0.6 0.0 copy-start
  0.6 0.0 copy-start.1
  0.7 1.3 %shard_map.111 = f32[64,256]{1,0:T(8,128)S(1)} custom-call(bf16[2,64,512]{2,1,0:T(8,128)(2,1)} %bitcast.4, bf16[2,512,256]{2,1,0:T(8,128)(2,1)} %comp.3), custom_call_target="tpu_custom_call" | custom-call | flops 16777216 | bytes 327680 | tf_op jit(solution)/shard_map/pallas_call | solution.py:171
  1.9 0.5 %collective-permute-start = (f32[64,256]{1,0:T(8,128)S(1)}, f32[64,256]{1,0:T(8,128)S(1)}, u32[]{:S(2)}, u32[]{:S(2)}) collective-permute-start(f32[64,256]{1,0:T(8,128)S(1)} %shard_map.111), channel_id=1, source_target_pairs={{0,1},{1,0},{2,3},{3,2},{4,5},{5,4},{6,7},{7,6},{8,9},{9,8},{10,11... | collective-permute-start | bytes 196616 | tf_op jit(solution)/shard_map/ppermute | solution.py:116
  2.4 0.0 copy-done
  2.4 0.0 copy-done.1
  2.5 0.0 copy-start.2
  2.5 0.0 copy-start.3
  2.5 0.9 %shard_map.110 = (f32[64,256]{1,0:T(8,128)S(1)}, f32[64,1]{1,0:T(8,128)S(1)}) custom-call(bf16[2,64,512]{2,1,0:T(8,128)(2,1)S(1)} %bitcast.5, bf16[2,512,256]{2,1,0:T(8,128)(2,1)S(1)} %copy-done, s32[1,64]{1,0:T(1,128)} %bitcast.8), custom_call_target="tpu_custom_call" | custom-call | flops 16777216 | bytes 327680 | tf_op jit(solution)/shard_map/pallas_call | solution.py:184
  3.3 0.0 collective-permute-done
  3.4 3.9 %collective-permute-start.3 = (f32[64,256]{1,0:T(8,128)S(1)}, f32[64,256]{1,0:T(8,128)S(1)}, u32[]{:S(2)}, u32[]{:S(2)}) collective-permute-start(f32[64,256]{1,0:T(8,128)S(1)} %add.15), channel_id=1, source_target_pairs={{0,6},{1,7},{2,4},{3,5},{4,2},{5,3},{6,0},{7,1},{8,14},{9,15},{10,... | collective-permute-start | bytes 196616 | tf_op jit(solution)/shard_map/ppermute | solution.py:116
  7.3 0.4 %collective-permute-start.2 = (f32[64,256]{1,0:T(8,128)S(1)}, f32[64,256]{1,0:T(8,128)S(1)}, u32[]{:S(2)}, u32[]{:S(2)}) collective-permute-start(f32[64,256]{1,0:T(8,128)S(1)} %add.15), channel_id=1, source_target_pairs={{0,4},{1,5},{2,6},{3,7},{4,0},{5,1},{6,2},{7,3},{8,12},{9,13},{10,... | collective-permute-start | bytes 196616 | tf_op jit(solution)/shard_map/ppermute | solution.py:116
  7.8 0.2 collective-permute-start.1
  8.0 1.8 %collective-permute-done.3 = f32[64,256]{1,0:T(8,128)S(1)} collective-permute-done((f32[64,256]{1,0:T(8,128)S(1)}, f32[64,256]{1,0:T(8,128)S(1)}, u32[]{:S(2)}, u32[]{:S(2)}) %collective-permute-start.3) | collective-permute-done | bytes 65568 | tf_op jit(solution)/shard_map/ppermute | solution.py:116
  9.7 1.9 %collective-permute-done.2 = f32[64,256]{1,0:T(8,128)S(1)} collective-permute-done((f32[64,256]{1,0:T(8,128)S(1)}, f32[64,256]{1,0:T(8,128)S(1)}, u32[]{:S(2)}, u32[]{:S(2)}) %collective-permute-start.2) | collective-permute-done | bytes 65568 | tf_op jit(solution)/shard_map/ppermute | solution.py:116
  11.6 0.4 %collective-permute-done.1 = f32[64,256]{1,0:T(8,128)S(1)} collective-permute-done((f32[64,256]{1,0:T(8,128)S(1)}, f32[64,256]{1,0:T(8,128)S(1)}, u32[]{:S(2)}, u32[]{:S(2)}) %collective-permute-start.1) | collective-permute-done | bytes 65568 | tf_op jit(solution)/shard_map/ppermute | solution.py:116
  12.0 0.0 copy-start.5
  12.1 2.7 %collective-permute-start.4 = (f32[64,256]{1,0:T(8,128)S(1)}, f32[64,256]{1,0:T(8,128)S(1)}, u32[]{:S(2)}, u32[]{:S(2)}) collective-permute-start(f32[64,256]{1,0:T(8,128)S(1)} %add_add_fusion), channel_id=1, source_target_pairs={{0,8},{1,9},{2,10},{3,11},{4,12},{5,13},{6,14},{7,15},{8,0},{9,1},... | collective-permute-start | bytes 196616 | tf_op jit(solution)/shard_map/ppermute | solution.py:116
  14.7 2.6 %collective-permute-done.4 = f32[64,256]{1,0:T(8,128)S(1)} collective-permute-done((f32[64,256]{1,0:T(8,128)S(1)}, f32[64,256]{1,0:T(8,128)S(1)}, u32[]{:S(2)}, u32[]{:S(2)}) %collective-permute-start.4) | collective-permute-done | bytes 65568 | tf_op jit(solution)/shard_map/ppermute | solution.py:116
  17.3 0.0 copy-start.4
  17.3 0.1 collective-permute-start.7
  17.4 1.6 %collective-permute-start.6 = (bf16[64,256]{1,0:T(8,128)(2,1)S(1)}, bf16[64,256]{1,0:T(8,128)(2,1)S(1)}, u32[]{:S(2)}, u32[]{:S(2)}) collective-permute-start(bf16[64,256]{1,0:T(8,128)(2,1)S(1)} %add_convert_fusion.mine), channel_id=1, source_target_pairs={{0,16},{1,17},{2,18},{3,19},{4,20},{5,21},{6,22},{7,23},{8,24},{9,... | collective-permute-start | bytes 98312 | tf_op jit(solution)/shard_map/ppermute | solution.py:116
  18.9 0.3 %collective-permute-start.5 = (bf16[64,256]{1,0:T(8,128)(2,1)S(1)}, bf16[64,256]{1,0:T(8,128)(2,1)S(1)}, u32[]{:S(2)}, u32[]{:S(2)}) collective-permute-start(bf16[64,256]{1,0:T(8,128)(2,1)S(1)} %add_convert_fusion.mine), channel_id=1, source_target_pairs={{0,1},{1,0},{2,3},{3,2},{4,5},{5,4},{6,7},{7,6},{8,9},{9,8},{10,11... | collective-permute-start | bytes 98312 | tf_op jit(solution)/shard_map/ppermute | solution.py:116
  19.2 0.0 copy-done.5
  19.2 1.8 %collective-permute-done.7.both_piece = bf16[64,256]{1,0:T(8,128)(2,1)S(1)} collective-permute-done((bf16[64,256]{1,0:T(8,128)(2,1)S(1)}, bf16[64,256]{1,0:T(8,128)(2,1)S(1)}, u32[]{:S(2)}, u32[]{:S(2)}) %collective-permute-start.7) | collective-permute-done | bytes 32800 | tf_op jit(solution)/shard_map/ppermute | solution.py:116
  21.0 0.4 %collective-permute-done.6.tower_piece = bf16[64,256]{1,0:T(8,128)(2,1)S(1)} collective-permute-done((bf16[64,256]{1,0:T(8,128)(2,1)S(1)}, bf16[64,256]{1,0:T(8,128)(2,1)S(1)}, u32[]{:S(2)}, u32[]{:S(2)}) %collective-permute-start.6) | collective-permute-done | bytes 32800 | tf_op jit(solution)/shard_map/ppermute | solution.py:116
  21.4 0.0 collective-permute-done.5.side_piece
  21.4 0.0 copy-done.2
  21.4 0.0 copy-done.3
  21.4 0.0 copy-done.4
  21.4 2.0 %shard_map.112 = (f32[2,512,256]{2,1,0:T(8,128)}, bf16[2,64,512]{2,1,0:T(8,128)(2,1)}, f32[32,256]{1,0:T(8,128)}, f32[32,256]{1,0:T(8,128)}, f32[2,32]{1,0:T(2,128)}) custom-call(bf16[64,256]{1,0:T(8,128)(2,1)S(1)} %add_convert_fusion.mine, bf16[64,256]{1,0:T(8,128)(2,1)S(1)} %collective-permute-done.5.side_piece, ...), custom_call_target="tpu_custom_call" | custom-call | flops 167772160 | bytes 4194304 | tf_op jit(solution)/shard_map/pallas_call | solution.py:304
  (4 shorter events, 0.0 us)
Async XLA Ops:
  0.6 1.8 %copy-start = (bf16[2,512,256]{2,1,0:T(8,128)(2,1)S(1)}, bf16[2,512,256]{2,1,0:T(8,128)(2,1)}, u32[]{:S(2)}) copy-start(bf16[2,512,256]{2,1,0:T(8,128)(2,1)} %comp.3) | copy-start | bytes 1572868
  0.6 1.8 %copy-start.1 = (bf16[2,512,64]{1,2,0:T(8,128)(2,1)S(1)}, bf16[2,512,64]{1,2,0:T(8,128)(2,1)}, u32[]{:S(2)}) copy-start(bf16[2,512,64]{1,2,0:T(8,128)(2,1)} %param.7) | copy-start | bytes 393220
  1.9 1.4 %collective-permute-start = (f32[64,256]{1,0:T(8,128)S(1)}, f32[64,256]{1,0:T(8,128)S(1)}, u32[]{:S(2)}, u32[]{:S(2)}) collective-permute-start(f32[64,256]{1,0:T(8,128)S(1)} %shard_map.111), channel_id=1, source_target_pairs={{0,1},{1,0},{2,3},{3,2},{4,5},{5,4},{6,7},{7,6},{8,9},{9,8},{10,11... | collective-permute-start | bytes 196616 | tf_op jit(solution)/shard_map/ppermute | solution.py:116
  2.5 19.0 %copy-start.2 = (bf16[1024,256]{1,0:T(8,128)(2,1)S(1)}, bf16[1024,256]{1,0:T(8,128)(2,1)}, u32[]{:S(2)}) copy-start(bf16[1024,256]{1,0:T(8,128)(2,1)} %down.1) | copy-start | bytes 1572868
  2.5 19.0 %copy-start.3 = (bf16[1024,256]{1,0:T(8,128)(2,1)S(1)}, bf16[1024,256]{1,0:T(8,128)(2,1)}, u32[]{:S(2)}) copy-start(bf16[1024,256]{1,0:T(8,128)(2,1)} %upper.1) | copy-start | bytes 1572868
  3.4 6.4 %collective-permute-start.3 = (f32[64,256]{1,0:T(8,128)S(1)}, f32[64,256]{1,0:T(8,128)S(1)}, u32[]{:S(2)}, u32[]{:S(2)}) collective-permute-start(f32[64,256]{1,0:T(8,128)S(1)} %add.15), channel_id=1, source_target_pairs={{0,6},{1,7},{2,4},{3,5},{4,2},{5,3},{6,0},{7,1},{8,14},{9,15},{10,... | collective-permute-start | bytes 196616 | tf_op jit(solution)/shard_map/ppermute | solution.py:116
  7.3 4.3 %collective-permute-start.2 = (f32[64,256]{1,0:T(8,128)S(1)}, f32[64,256]{1,0:T(8,128)S(1)}, u32[]{:S(2)}, u32[]{:S(2)}) collective-permute-start(f32[64,256]{1,0:T(8,128)S(1)} %add.15), channel_id=1, source_target_pairs={{0,4},{1,5},{2,6},{3,7},{4,0},{5,1},{6,2},{7,3},{8,12},{9,13},{10,... | collective-permute-start | bytes 196616 | tf_op jit(solution)/shard_map/ppermute | solution.py:116
  7.8 4.3 %collective-permute-start.1 = (f32[64,256]{1,0:T(8,128)S(1)}, f32[64,256]{1,0:T(8,128)S(1)}, u32[]{:S(2)}, u32[]{:S(2)}) collective-permute-start(f32[64,256]{1,0:T(8,128)S(1)} %add.15), channel_id=1, source_target_pairs={{0,2},{1,3},{2,0},{3,1},{4,6},{5,7},{6,4},{7,5},{8,10},{9,11},{10,... | collective-permute-start | bytes 196616 | tf_op jit(solution)/shard_map/ppermute | solution.py:116
  12.0 7.2 %copy-start.5 = (bf16[1024]{0:T(1024)(128)(2,1)S(1)}, bf16[1024]{0:T(1024)(128)(2,1)}, u32[]{:S(2)}) copy-start(bf16[1024]{0:T(1024)(128)(2,1)} %param.12) | copy-start | bytes 6148
  12.1 5.2 %collective-permute-start.4 = (f32[64,256]{1,0:T(8,128)S(1)}, f32[64,256]{1,0:T(8,128)S(1)}, u32[]{:S(2)}, u32[]{:S(2)}) collective-permute-start(f32[64,256]{1,0:T(8,128)S(1)} %add_add_fusion), channel_id=1, source_target_pairs={{0,8},{1,9},{2,10},{3,11},{4,12},{5,13},{6,14},{7,15},{8,0},{9,1},... | collective-permute-start | bytes 196616 | tf_op jit(solution)/shard_map/ppermute | solution.py:116
  17.3 4.1 %copy-start.4 = (f32[1024]{0:T(1024)S(1)}, f32[1024]{0:T(1024)}, u32[]{:S(2)}) copy-start(f32[1024]{0:T(1024)} %param.11) | copy-start | bytes 12292
  17.3 3.7 %collective-permute-start.7 = (bf16[64,256]{1,0:T(8,128)(2,1)S(1)}, bf16[64,256]{1,0:T(8,128)(2,1)S(1)}, u32[]{:S(2)}, u32[]{:S(2)}) collective-permute-start(bf16[64,256]{1,0:T(8,128)(2,1)S(1)} %add_convert_fusion.mine), channel_id=1, source_target_pairs={{0,17},{1,16},{2,19},{3,18},{4,21},{5,20},{6,23},{7,22},{8,25},{9,... | collective-permute-start | bytes 98312 | tf_op jit(solution)/shard_map/ppermute | solution.py:116
  17.4 4.0 %collective-permute-start.6 = (bf16[64,256]{1,0:T(8,128)(2,1)S(1)}, bf16[64,256]{1,0:T(8,128)(2,1)S(1)}, u32[]{:S(2)}, u32[]{:S(2)}) collective-permute-start(bf16[64,256]{1,0:T(8,128)(2,1)S(1)} %add_convert_fusion.mine), channel_id=1, source_target_pairs={{0,16},{1,17},{2,18},{3,19},{4,20},{5,21},{6,22},{7,23},{8,24},{9,... | collective-permute-start | bytes 98312 | tf_op jit(solution)/shard_map/ppermute | solution.py:116
  18.9 2.5 %collective-permute-start.5 = (bf16[64,256]{1,0:T(8,128)(2,1)S(1)}, bf16[64,256]{1,0:T(8,128)(2,1)S(1)}, u32[]{:S(2)}, u32[]{:S(2)}) collective-permute-start(bf16[64,256]{1,0:T(8,128)(2,1)S(1)} %add_convert_fusion.mine), channel_id=1, source_target_pairs={{0,1},{1,0},{2,3},{3,2},{4,5},{5,4},{6,7},{7,6},{8,9},{9,8},{10,11... | collective-permute-start | bytes 98312 | tf_op jit(solution)/shard_map/ppermute | solution.py:116

commit v5 on v4

--- a/solution.py
+++ b/solution.py
@@ -299,7 +299,7 @@
         one, two = strides.pop(0), strides.pop(0)
         total = total + sum(exchange(total, 0, bits) for bits in (one, two, one | two))
     for stride in strides:
-        total = total + exchange(total, 0, stride)
+        total = total + exchange(total.astype(BF16), 0, stride).astype(F32)
     mine = total.astype(BF16)
     grad_w, grad_x, grad_down, grad_up, vectors = pl.pallas_call(
         top_kernel,

time: 23.6 us -> 23.3 us (0.987)
  waiting for transfers between devices: 8.84 us -> 8.49 us
    ppermute x8, waiting for transfers between devices: 8.84 us -> 8.49 us  [exchange(): return lax.ppermute(value, ('tower', 'member'), pairs)]
where the time goes in v5:
time: 23.3 us; the launch traced here: 23.1 us
  starting transfers between devices  9.68 us (42%)
  waiting for transfers between devices  8.49 us (36%)
  Pallas kernels  4.15 us (18%)
  between operations  0.72 us (3%)
    ppermute x8, starting transfers between devices, exchange(): return lax.ppermute(value, ('tower', 'member'), pairs)  9.68 us
    ppermute x8, waiting for transfers between devices, exchange(): return lax.ppermute(value, ('tower', 'member'), pairs)  8.49 us
    pallas_call x1, Pallas kernels, shards_doubling(): pl.pallas_call(top_kernel, out_shape=(jax.ShapeDtypeStruct((local_towers,...  2.02 us
    pallas_call x1, Pallas kernels, terms(): pl.pallas_call(sent_kernel, out_shape=jax.ShapeDtypeStruct((batch, width)...  1.27 us
    pallas_call x1, Pallas kernels, terms(): pl.pallas_call(kept_kernel, out_shape=(jax.ShapeDtypeStruct((batch, width...  0.86 us
  transfers between devices with their start and end apart: 8, of which 6 were waited for; matrix products, arithmetic and copies ran while one was open for 0% of the time, Pallas kernels for 4%

profile of v5, /device:TPU:0, one launch (start us, length us, event | category | flops | bytes accessed | tf_op | source)
XLA Modules:
  0.0 23.1 jit_solution(15691100592867514107)
XLA Ops:
  0.6 0.0 copy-start
  0.6 0.0 copy-start.1
  0.7 1.3 %shard_map.111 = f32[64,256]{1,0:T(8,128)S(1)} custom-call(bf16[2,64,512]{2,1,0:T(8,128)(2,1)} %bitcast.4, bf16[2,512,256]{2,1,0:T(8,128)(2,1)} %comp.3), custom_call_target="tpu_custom_call" | custom-call | flops 16777216 | bytes 327680 | tf_op jit(solution)/shard_map/pallas_call | solution.py:171
  1.9 0.5 %collective-permute-start = (f32[64,256]{1,0:T(8,128)S(1)}, f32[64,256]{1,0:T(8,128)S(1)}, u32[]{:S(2)}, u32[]{:S(2)}) collective-permute-start(f32[64,256]{1,0:T(8,128)S(1)} %shard_map.111), channel_id=1, source_target_pairs={{0,1},{1,0},{2,3},{3,2},{4,5},{5,4},{6,7},{7,6},{8,9},{9,8},{10,11... | collective-permute-start | bytes 196616 | tf_op jit(solution)/shard_map/ppermute | solution.py:116
  2.4 0.0 copy-done
  2.4 0.0 copy-done.1
  2.5 0.0 copy-start.2
  2.5 0.0 copy-start.3
  2.5 0.9 %shard_map.110 = (f32[64,256]{1,0:T(8,128)S(1)}, f32[64,1]{1,0:T(8,128)S(1)}) custom-call(bf16[2,64,512]{2,1,0:T(8,128)(2,1)S(1)} %bitcast.5, bf16[2,512,256]{2,1,0:T(8,128)(2,1)S(1)} %copy-done, s32[1,64]{1,0:T(1,128)} %bitcast.8), custom_call_target="tpu_custom_call" | custom-call | flops 16777216 | bytes 327680 | tf_op jit(solution)/shard_map/pallas_call | solution.py:184
  3.3 0.0 collective-permute-done
  3.4 3.9 %collective-permute-start.3 = (f32[64,256]{1,0:T(8,128)S(1)}, f32[64,256]{1,0:T(8,128)S(1)}, u32[]{:S(2)}, u32[]{:S(2)}) collective-permute-start(f32[64,256]{1,0:T(8,128)S(1)} %add.15), channel_id=1, source_target_pairs={{0,6},{1,7},{2,4},{3,5},{4,2},{5,3},{6,0},{7,1},{8,14},{9,15},{10,... | collective-permute-start | bytes 196616 | tf_op jit(solution)/shard_map/ppermute | solution.py:116
  7.3 0.4 %collective-permute-start.2 = (f32[64,256]{1,0:T(8,128)S(1)}, f32[64,256]{1,0:T(8,128)S(1)}, u32[]{:S(2)}, u32[]{:S(2)}) collective-permute-start(f32[64,256]{1,0:T(8,128)S(1)} %add.15), channel_id=1, source_target_pairs={{0,4},{1,5},{2,6},{3,7},{4,0},{5,1},{6,2},{7,3},{8,12},{9,13},{10,... | collective-permute-start | bytes 196616 | tf_op jit(solution)/shard_map/ppermute | solution.py:116
  7.8 0.2 collective-permute-start.1
  8.0 1.8 %collective-permute-done.3 = f32[64,256]{1,0:T(8,128)S(1)} collective-permute-done((f32[64,256]{1,0:T(8,128)S(1)}, f32[64,256]{1,0:T(8,128)S(1)}, u32[]{:S(2)}, u32[]{:S(2)}) %collective-permute-start.3) | collective-permute-done | bytes 65568 | tf_op jit(solution)/shard_map/ppermute | solution.py:116
  9.7 1.9 %collective-permute-done.2 = f32[64,256]{1,0:T(8,128)S(1)} collective-permute-done((f32[64,256]{1,0:T(8,128)S(1)}, f32[64,256]{1,0:T(8,128)S(1)}, u32[]{:S(2)}, u32[]{:S(2)}) %collective-permute-start.2) | collective-permute-done | bytes 65568 | tf_op jit(solution)/shard_map/ppermute | solution.py:116
  11.6 0.4 %collective-permute-done.1 = f32[64,256]{1,0:T(8,128)S(1)} collective-permute-done((f32[64,256]{1,0:T(8,128)S(1)}, f32[64,256]{1,0:T(8,128)S(1)}, u32[]{:S(2)}, u32[]{:S(2)}) %collective-permute-start.1) | collective-permute-done | bytes 65568 | tf_op jit(solution)/shard_map/ppermute | solution.py:116
  12.0 2.7 %collective-permute-start.4 = (bf16[64,256]{1,0:T(8,128)(2,1)S(1)}, bf16[64,256]{1,0:T(8,128)(2,1)S(1)}, u32[]{:S(2)}, u32[]{:S(2)}) collective-permute-start(bf16[64,256]{1,0:T(8,128)(2,1)S(1)} %get-tuple-element.19), channel_id=1, source_target_pairs={{0,8},{1,9},{2,10},{3,11},{4,12},{5,13},{6,14},{7,15},{8,0},{9,1},... | collective-permute-start | bytes 98312 | tf_op jit(solution)/shard_map/ppermute | solution.py:116
  14.7 2.2 %collective-permute-done.4 = bf16[64,256]{1,0:T(8,128)(2,1)S(1)} collective-permute-done((bf16[64,256]{1,0:T(8,128)(2,1)S(1)}, bf16[64,256]{1,0:T(8,128)(2,1)S(1)}, u32[]{:S(2)}, u32[]{:S(2)}) %collective-permute-start.4) | collective-permute-done | bytes 32800 | tf_op jit(solution)/shard_map/ppermute | solution.py:116
  16.9 0.0 copy-start.5
  16.9 0.0 copy-start.4
  16.9 0.1 collective-permute-start.7
  17.0 1.6 %collective-permute-start.6 = (bf16[64,256]{1,0:T(8,128)(2,1)S(1)}, bf16[64,256]{1,0:T(8,128)(2,1)S(1)}, u32[]{:S(2)}, u32[]{:S(2)}) collective-permute-start(bf16[64,256]{1,0:T(8,128)(2,1)S(1)} %add_convert_fusion.mine), channel_id=1, source_target_pairs={{0,16},{1,17},{2,18},{3,19},{4,20},{5,21},{6,22},{7,23},{8,24},{9,... | collective-permute-start | bytes 98312 | tf_op jit(solution)/shard_map/ppermute | solution.py:116
  18.6 0.3 %collective-permute-start.5 = (bf16[64,256]{1,0:T(8,128)(2,1)S(1)}, bf16[64,256]{1,0:T(8,128)(2,1)S(1)}, u32[]{:S(2)}, u32[]{:S(2)}) collective-permute-start(bf16[64,256]{1,0:T(8,128)(2,1)S(1)} %add_convert_fusion.mine), channel_id=1, source_target_pairs={{0,1},{1,0},{2,3},{3,2},{4,5},{5,4},{6,7},{7,6},{8,9},{9,8},{10,11... | collective-permute-start | bytes 98312 | tf_op jit(solution)/shard_map/ppermute | solution.py:116
  18.9 0.0 copy-done.5
  18.9 1.8 %collective-permute-done.7.both_piece = bf16[64,256]{1,0:T(8,128)(2,1)S(1)} collective-permute-done((bf16[64,256]{1,0:T(8,128)(2,1)S(1)}, bf16[64,256]{1,0:T(8,128)(2,1)S(1)}, u32[]{:S(2)}, u32[]{:S(2)}) %collective-permute-start.7) | collective-permute-done | bytes 32800 | tf_op jit(solution)/shard_map/ppermute | solution.py:116
  20.7 0.4 %collective-permute-done.6.tower_piece = bf16[64,256]{1,0:T(8,128)(2,1)S(1)} collective-permute-done((bf16[64,256]{1,0:T(8,128)(2,1)S(1)}, bf16[64,256]{1,0:T(8,128)(2,1)S(1)}, u32[]{:S(2)}, u32[]{:S(2)}) %collective-permute-start.6) | collective-permute-done | bytes 32800 | tf_op jit(solution)/shard_map/ppermute | solution.py:116
  21.1 0.0 collective-permute-done.5.side_piece
  21.1 0.0 copy-done.2
  21.1 0.0 copy-done.3
  21.1 0.0 copy-done.4
  21.1 2.0 %shard_map.112 = (f32[2,512,256]{2,1,0:T(8,128)}, bf16[2,64,512]{2,1,0:T(8,128)(2,1)}, f32[32,256]{1,0:T(8,128)}, f32[32,256]{1,0:T(8,128)}, f32[2,32]{1,0:T(2,128)}) custom-call(bf16[64,256]{1,0:T(8,128)(2,1)S(1)} %add_convert_fusion.mine, bf16[64,256]{1,0:T(8,128)(2,1)S(1)} %collective-permute-done.5.side_piece, ...), custom_call_target="tpu_custom_call" | custom-call | flops 167772160 | bytes 4194304 | tf_op jit(solution)/shard_map/pallas_call | solution.py:304
  (4 shorter events, 0.0 us)
Async XLA Ops:
  0.6 1.8 %copy-start = (bf16[2,512,256]{2,1,0:T(8,128)(2,1)S(1)}, bf16[2,512,256]{2,1,0:T(8,128)(2,1)}, u32[]{:S(2)}) copy-start(bf16[2,512,256]{2,1,0:T(8,128)(2,1)} %comp.3) | copy-start | bytes 1572868
  0.6 1.8 %copy-start.1 = (bf16[2,512,64]{1,2,0:T(8,128)(2,1)S(1)}, bf16[2,512,64]{1,2,0:T(8,128)(2,1)}, u32[]{:S(2)}) copy-start(bf16[2,512,64]{1,2,0:T(8,128)(2,1)} %param.7) | copy-start | bytes 393220
  1.9 1.4 %collective-permute-start = (f32[64,256]{1,0:T(8,128)S(1)}, f32[64,256]{1,0:T(8,128)S(1)}, u32[]{:S(2)}, u32[]{:S(2)}) collective-permute-start(f32[64,256]{1,0:T(8,128)S(1)} %shard_map.111), channel_id=1, source_target_pairs={{0,1},{1,0},{2,3},{3,2},{4,5},{5,4},{6,7},{7,6},{8,9},{9,8},{10,11... | collective-permute-start | bytes 196616 | tf_op jit(solution)/shard_map/ppermute | solution.py:116
  2.5 18.6 %copy-start.2 = (bf16[1024,256]{1,0:T(8,128)(2,1)S(1)}, bf16[1024,256]{1,0:T(8,128)(2,1)}, u32[]{:S(2)}) copy-start(bf16[1024,256]{1,0:T(8,128)(2,1)} %down.1) | copy-start | bytes 1572868
  2.5 18.6 %copy-start.3 = (bf16[1024,256]{1,0:T(8,128)(2,1)S(1)}, bf16[1024,256]{1,0:T(8,128)(2,1)}, u32[]{:S(2)}) copy-start(bf16[1024,256]{1,0:T(8,128)(2,1)} %upper.1) | copy-start | bytes 1572868
  3.4 6.4 %collective-permute-start.3 = (f32[64,256]{1,0:T(8,128)S(1)}, f32[64,256]{1,0:T(8,128)S(1)}, u32[]{:S(2)}, u32[]{:S(2)}) collective-permute-start(f32[64,256]{1,0:T(8,128)S(1)} %add.15), channel_id=1, source_target_pairs={{0,6},{1,7},{2,4},{3,5},{4,2},{5,3},{6,0},{7,1},{8,14},{9,15},{10,... | collective-permute-start | bytes 196616 | tf_op jit(solution)/shard_map/ppermute | solution.py:116
  7.3 4.3 %collective-permute-start.2 = (f32[64,256]{1,0:T(8,128)S(1)}, f32[64,256]{1,0:T(8,128)S(1)}, u32[]{:S(2)}, u32[]{:S(2)}) collective-permute-start(f32[64,256]{1,0:T(8,128)S(1)} %add.15), channel_id=1, source_target_pairs={{0,4},{1,5},{2,6},{3,7},{4,0},{5,1},{6,2},{7,3},{8,12},{9,13},{10,... | collective-permute-start | bytes 196616 | tf_op jit(solution)/shard_map/ppermute | solution.py:116
  7.8 4.3 %collective-permute-start.1 = (f32[64,256]{1,0:T(8,128)S(1)}, f32[64,256]{1,0:T(8,128)S(1)}, u32[]{:S(2)}, u32[]{:S(2)}) collective-permute-start(f32[64,256]{1,0:T(8,128)S(1)} %add.15), channel_id=1, source_target_pairs={{0,2},{1,3},{2,0},{3,1},{4,6},{5,7},{6,4},{7,5},{8,10},{9,11},{10,... | collective-permute-start | bytes 196616 | tf_op jit(solution)/shard_map/ppermute | solution.py:116
  12.0 4.9 %collective-permute-start.4 = (bf16[64,256]{1,0:T(8,128)(2,1)S(1)}, bf16[64,256]{1,0:T(8,128)(2,1)S(1)}, u32[]{:S(2)}, u32[]{:S(2)}) collective-permute-start(bf16[64,256]{1,0:T(8,128)(2,1)S(1)} %get-tuple-element.19), channel_id=1, source_target_pairs={{0,8},{1,9},{2,10},{3,11},{4,12},{5,13},{6,14},{7,15},{8,0},{9,1},... | collective-permute-start | bytes 98312 | tf_op jit(solution)/shard_map/ppermute | solution.py:116
  16.9 2.0 %copy-start.5 = (bf16[1024]{0:T(1024)(128)(2,1)S(1)}, bf16[1024]{0:T(1024)(128)(2,1)}, u32[]{:S(2)}) copy-start(bf16[1024]{0:T(1024)(128)(2,1)} %param.12) | copy-start | bytes 6148
  16.9 4.1 %copy-start.4 = (f32[1024]{0:T(1024)S(1)}, f32[1024]{0:T(1024)}, u32[]{:S(2)}) copy-start(f32[1024]{0:T(1024)} %param.11) | copy-start | bytes 12292
  16.9 3.7 %collective-permute-start.7 = (bf16[64,256]{1,0:T(8,128)(2,1)S(1)}, bf16[64,256]{1,0:T(8,128)(2,1)S(1)}, u32[]{:S(2)}, u32[]{:S(2)}) collective-permute-start(bf16[64,256]{1,0:T(8,128)(2,1)S(1)} %add_convert_fusion.mine), channel_id=1, source_target_pairs={{0,17},{1,16},{2,19},{3,18},{4,21},{5,20},{6,23},{7,22},{8,25},{9,... | collective-permute-start | bytes 98312 | tf_op jit(solution)/shard_map/ppermute | solution.py:116
  17.0 4.0 %collective-permute-start.6 = (bf16[64,256]{1,0:T(8,128)(2,1)S(1)}, bf16[64,256]{1,0:T(8,128)(2,1)S(1)}, u32[]{:S(2)}, u32[]{:S(2)}) collective-permute-start(bf16[64,256]{1,0:T(8,128)(2,1)S(1)} %add_convert_fusion.mine), channel_id=1, source_target_pairs={{0,16},{1,17},{2,18},{3,19},{4,20},{5,21},{6,22},{7,23},{8,24},{9,... | collective-permute-start | bytes 98312 | tf_op jit(solution)/shard_map/ppermute | solution.py:116
  18.6 2.5 %collective-permute-start.5 = (bf16[64,256]{1,0:T(8,128)(2,1)S(1)}, bf16[64,256]{1,0:T(8,128)(2,1)S(1)}, u32[]{:S(2)}, u32[]{:S(2)}) collective-permute-start(bf16[64,256]{1,0:T(8,128)(2,1)S(1)} %add_convert_fusion.mine), channel_id=1, source_target_pairs={{0,1},{1,0},{2,3},{3,2},{4,5},{5,4},{6,7},{7,6},{8,9},{9,8},{10,11... | collective-permute-start | bytes 98312 | tf_op jit(solution)/shard_map/ppermute | solution.py:116

commit v6 on v5

--- a/solution.py
+++ b/solution.py
@@ -196,49 +196,62 @@
     return sent, kept, target
 
 
+def products(pieces, down, upper, bias, wout, order):
+    low = back = score = None
+    width = pieces[0].shape[1]
+    for piece, j in zip(pieces, order):
+        rows = pl.ds(pl.multiple_of(j * width, width), width)
+        scaled = piece.astype(F32) * wout[j]
+        parts = (
+            jnp.dot(piece, down[rows, :], preferred_element_type=F32),
+            jnp.dot(scaled.astype(BF16), upper[rows, :], preferred_element_type=F32),
+            scaled * (bias[j] + 1.0),
+        )
+        if low is None:
+            low, back, score = parts
+        else:
+            low, back, score = low + parts[0], back + parts[1], score + parts[2]
+    return low, back, score
+
+
+def near_kernel(mine, down, upper, bias, wout, low, back, score):
+    tower = lax.axis_index("tower")
+    side = side_of(lax.axis_index("member"))
+    low[...], back[...], score[...] = products(
+        (mine[...],), down, upper, bias, wout, (2 * tower + side,)
+    )
+
+
 def top_kernel(
-    mine, side_piece, tower_piece, both_piece, down, upper, bias, wout, target, feat, comp,
+    mine, side_piece, tower_piece, both_piece, near_low, near_back, near_score,
+    down, upper, bias, wout, target, feat, comp,
     grad_w_hbm, grad_x_hbm, grad_down_hbm, grad_up_hbm, vectors_hbm,
-    compressed, gates, wide, grad_w, grad_x, up_square, down_square, vectors, sems,
+    compressed, gates, grad_w, grad_x, up_square, down_square, vectors, sems,
 ):
     tower, member = lax.axis_index("tower"), lax.axis_index("member")
     side = side_of(member)
     batch, width = mine.shape
-    pieces = compressed.shape[0]
-    compressed[2 * tower + side] = mine[...]
-    compressed[2 * tower + 1 - side] = side_piece[...]
-    compressed[2 * (1 - tower) + side] = tower_piece[...]
-    compressed[2 * (1 - tower) + 1 - side] = both_piece[...]
-    block = lambda j: slice(j * width, (j + 1) * width)
-    summed = lambda parts: functools.reduce(jnp.add, parts)
-
-    low = summed(
-        jnp.dot(compressed[j], down[block(j), :], preferred_element_type=F32)
-        for j in range(pieces)
-    ).astype(BF16)
-    weighted = [
-        (compressed[j].astype(F32) * wout[:, block(j)].astype(F32)).astype(BF16)
-        for j in range(pieces)
-    ]
-    back = summed(
-        jnp.dot(weighted[j], upper[block(j), :], preferred_element_type=F32)
-        for j in range(pieces)
-    )
-    back_low = back.astype(BF16)
-    scores = []
-    for j in range(pieces):
-        gate = nt(low, upper[block(j), :]) + bias[:, block(j)]
-        gates[j] = gate
-        out_row = wout[:, block(j)].astype(F32)
-        wide[j] = out_row
-        comp_f = compressed[j].astype(F32)
-        scores.append((comp_f * gate + comp_f) * out_row)
-    logit = jnp.sum(summed(scores), axis=1, keepdims=True)
+    compressed[side] = mine[...]
+    compressed[1 - side] = side_piece[...]
+    other = 2 * (1 - tower)
+    low_f, back, score = products(
+        (side_piece[...], tower_piece[...], both_piece[...]),
+        down,
+        upper,
+        bias,
+        wout,
+        (2 * tower + 1 - side, other + side, other + 1 - side),
+    )
+    low_f, back = near_low[...] + low_f, near_back[...] + back
+    low, back_low = low_f.astype(BF16), back.astype(BF16)
+    logit = jnp.sum(near_score[...] + score + low.astype(F32) * back, axis=1, keepdims=True)
     slopes = []
     for k in range(2):
         j = 2 * tower + k
         rows = pl.ds(pl.multiple_of(j * width, width), width)
-        slopes.append(wide[j] * (gates[j] + 1.0) + nt(back_low, down[rows, :]))
+        gate = nt(low, upper[rows, :]) + (bias[j] + 1.0)
+        gates[k] = gate
+        slopes.append(wout[j] * gate + nt(back_low, down[rows, :]))
     dlogit = 1.0 / (1.0 + jnp.exp(-logit)) - target[...]
 
     stores = []
@@ -260,11 +273,11 @@
 
     count = grad_down_hbm.shape[0]
     first = (tower * lax.axis_size("member") + member) * count
-    own = lax.div(first, width)
+    own = lax.div(first, width) - 2 * tower
     offset = pl.multiple_of(lax.rem(first, width), count)
     comp_f = compressed[own].astype(F32)
-    dgate_f = dlogit * wide[own] * comp_f
-    crossed = comp_f * gates[own] + comp_f
+    dgate_f = dlogit * wout[2 * tower + own] * comp_f
+    crossed = comp_f * gates[own]
     up_square[...] = contract_rows(dgate_f.astype(BF16), low)
     send(up_square.at[pl.ds(offset, count)], grad_up_hbm)
     down_square[...] = contract_rows(compressed[own], (dlogit * back).astype(BF16))
@@ -301,6 +314,25 @@
     for stride in strides:
         total = total + exchange(total.astype(BF16), 0, stride).astype(F32)
     mine = total.astype(BF16)
+    side_piece = exchange(mine, 0, 1)
+    tower_piece, both_piece = exchange(mine, 1, 0), exchange(mine, 1, 1)
+    weights = (
+        near(top_down),
+        near(top_up),
+        near(top_bias.reshape(pieces, 1, width)),
+        near(out_weight.astype(F32).reshape(pieces, 1, width)),
+    )
+    near_sums = pl.pallas_call(
+        near_kernel,
+        out_shape=(jax.ShapeDtypeStruct((batch, rank), F32),) * 2
+        + (jax.ShapeDtypeStruct((batch, width), F32),),
+        in_specs=[VMEM] * 5,
+        out_specs=(VMEM,) * 3,
+        compiler_params=pltpu.CompilerParams(vmem_limit_bytes=4 << 20),
+        cost_estimate=pl.CostEstimate(
+            flops=4 * batch * width * rank, bytes_accessed=1 << 20, transcendentals=0
+        ),
+    )(near(mine), *weights)
     grad_w, grad_x, grad_down, grad_up, vectors = pl.pallas_call(
         top_kernel,
         out_shape=(
@@ -310,12 +342,11 @@
             jax.ShapeDtypeStruct((count, rank), F32),
             jax.ShapeDtypeStruct((2, count), F32),
         ),
-        in_specs=[VMEM] * 11,
+        in_specs=[VMEM] * 14,
         out_specs=(ANY,) * 5,
         scratch_shapes=[
-            pltpu.VMEM((pieces, batch, width), BF16),
-            pltpu.VMEM((pieces, batch, width), F32),
-            pltpu.VMEM((pieces, 1, width), F32),
+            pltpu.VMEM((local_towers, batch, width), BF16),
+            pltpu.VMEM((local_towers, batch, width), F32),
             pltpu.VMEM((CHUNKS, local_towers * feat_rows // CHUNKS, width), F32),
             pltpu.VMEM((local_towers, batch, feat_rows), BF16),
             pltpu.VMEM((width, rank), F32),
@@ -329,13 +360,11 @@
         ),
     )(
         near(mine),
-        near(exchange(mine, 0, 1)),
-        near(exchange(mine, 1, 0)),
-        near(exchange(mine, 1, 1)),
-        near(top_down),
-        near(top_up),
-        near(top_bias.reshape(1, top)),
-        near(out_weight.reshape(1, top)),
+        near(side_piece),
+        near(tower_piece),
+        near(both_piece),
+        *(near(value) for value in near_sums),
+        *weights,
         near(target),
         near(feat_t),
         near(compress),

time: 23.3 us -> 23 us (0.987)
  transfers between devices with their start and end apart: 8 -> 8, of which waited for: 6 -> 6; matrix products, arithmetic and copies ran while one was open for 0% -> 0% of each run, Pallas kernels for 4% -> 5%
where the time goes in v6:
time: 23 us; the launch traced here: 22.8 us
  starting transfers between devices  9.68 us (42%)
  waiting for transfers between devices  8.3 us (36%)
  Pallas kernels  4.09 us (18%)
  between operations  0.72 us (3%)
    ppermute x8, starting transfers between devices, exchange(): return lax.ppermute(value, ('tower', 'member'), pairs)  9.68 us
    ppermute x8, waiting for transfers between devices, exchange(): return lax.ppermute(value, ('tower', 'member'), pairs)  8.3 us
    pallas_call x1, Pallas kernels, shards_doubling(): pl.pallas_call(top_kernel, out_shape=(jax.ShapeDtypeStruct((local_towers,...  1.79 us
    pallas_call x1, Pallas kernels, terms(): pl.pallas_call(sent_kernel, out_shape=jax.ShapeDtypeStruct((batch, width)...  1.27 us
    pallas_call x1, Pallas kernels, terms(): pl.pallas_call(kept_kernel, out_shape=(jax.ShapeDtypeStruct((batch, width...  0.86 us
  transfers between devices with their start and end apart: 8, of which 6 were waited for; matrix products, arithmetic and copies ran while one was open for 0% of the time, Pallas kernels for 5%

profile of v6, /device:TPU:0, one launch (start us, length us, event | category | flops | bytes accessed | tf_op | source)
XLA Modules:
  0.0 22.8 jit_solution(9439023939552284297)
XLA Ops:
  0.6 0.0 copy-start
  0.6 0.0 copy-start.3
  0.7 1.3 %shard_map.111 = f32[64,256]{1,0:T(8,128)S(1)} custom-call(bf16[2,64,512]{2,1,0:T(8,128)(2,1)} %bitcast.5, bf16[2,512,256]{2,1,0:T(8,128)(2,1)} %comp.3), custom_call_target="tpu_custom_call" | custom-call | flops 16777216 | bytes 327680 | tf_op jit(solution)/shard_map/pallas_call | solution.py:171
  1.9 0.5 %collective-permute-start = (f32[64,256]{1,0:T(8,128)S(1)}, f32[64,256]{1,0:T(8,128)S(1)}, u32[]{:S(2)}, u32[]{:S(2)}) collective-permute-start(f32[64,256]{1,0:T(8,128)S(1)} %shard_map.111), channel_id=1, source_target_pairs={{0,1},{1,0},{2,3},{3,2},{4,5},{5,4},{6,7},{7,6},{8,9},{9,8},{10,11... | collective-permute-start | bytes 196616 | tf_op jit(solution)/shard_map/ppermute | solution.py:116
  2.4 0.0 copy-done
  2.4 0.0 copy-done.3
  2.5 0.0 copy-start.1
  2.5 0.0 copy-start.2
  2.5 0.9 %shard_map.110 = (f32[64,256]{1,0:T(8,128)S(1)}, f32[64,1]{1,0:T(8,128)S(1)}) custom-call(bf16[2,64,512]{2,1,0:T(8,128)(2,1)S(1)} %bitcast.6, bf16[2,512,256]{2,1,0:T(8,128)(2,1)S(1)} %copy-done, s32[1,64]{1,0:T(1,128)} %bitcast.12), custom_call_target="tpu_custom_call" | custom-call | flops 16777216 | bytes 327680 | tf_op jit(solution)/shard_map/pallas_call | solution.py:184
  3.3 0.0 collective-permute-done
  3.4 3.9 %collective-permute-start.3 = (f32[64,256]{1,0:T(8,128)S(1)}, f32[64,256]{1,0:T(8,128)S(1)}, u32[]{:S(2)}, u32[]{:S(2)}) collective-permute-start(f32[64,256]{1,0:T(8,128)S(1)} %add.15), channel_id=1, source_target_pairs={{0,6},{1,7},{2,4},{3,5},{4,2},{5,3},{6,0},{7,1},{8,14},{9,15},{10,... | collective-permute-start | bytes 196616 | tf_op jit(solution)/shard_map/ppermute | solution.py:116
  7.3 0.4 %collective-permute-start.2 = (f32[64,256]{1,0:T(8,128)S(1)}, f32[64,256]{1,0:T(8,128)S(1)}, u32[]{:S(2)}, u32[]{:S(2)}) collective-permute-start(f32[64,256]{1,0:T(8,128)S(1)} %add.15), channel_id=1, source_target_pairs={{0,4},{1,5},{2,6},{3,7},{4,0},{5,1},{6,2},{7,3},{8,12},{9,13},{10,... | collective-permute-start | bytes 196616 | tf_op jit(solution)/shard_map/ppermute | solution.py:116
  7.8 0.2 collective-permute-start.1
  8.0 1.8 %collective-permute-done.3 = f32[64,256]{1,0:T(8,128)S(1)} collective-permute-done((f32[64,256]{1,0:T(8,128)S(1)}, f32[64,256]{1,0:T(8,128)S(1)}, u32[]{:S(2)}, u32[]{:S(2)}) %collective-permute-start.3) | collective-permute-done | bytes 65568 | tf_op jit(solution)/shard_map/ppermute | solution.py:116
  9.7 1.9 %collective-permute-done.2 = f32[64,256]{1,0:T(8,128)S(1)} collective-permute-done((f32[64,256]{1,0:T(8,128)S(1)}, f32[64,256]{1,0:T(8,128)S(1)}, u32[]{:S(2)}, u32[]{:S(2)}) %collective-permute-start.2) | collective-permute-done | bytes 65568 | tf_op jit(solution)/shard_map/ppermute | solution.py:116
  11.6 0.4 %collective-permute-done.1 = f32[64,256]{1,0:T(8,128)S(1)} collective-permute-done((f32[64,256]{1,0:T(8,128)S(1)}, f32[64,256]{1,0:T(8,128)S(1)}, u32[]{:S(2)}, u32[]{:S(2)}) %collective-permute-start.1) | collective-permute-done | bytes 65568 | tf_op jit(solution)/shard_map/ppermute | solution.py:116
  12.0 2.7 %collective-permute-start.4 = (bf16[64,256]{1,0:T(8,128)(2,1)S(1)}, bf16[64,256]{1,0:T(8,128)(2,1)S(1)}, u32[]{:S(2)}, u32[]{:S(2)}) collective-permute-start(bf16[64,256]{1,0:T(8,128)(2,1)S(1)} %get-tuple-element.25), channel_id=1, source_target_pairs={{0,8},{1,9},{2,10},{3,11},{4,12},{5,13},{6,14},{7,15},{8,0},{9,1},... | collective-permute-start | bytes 98312 | tf_op jit(solution)/shard_map/ppermute | solution.py:116
  14.7 2.2 %collective-permute-done.4 = bf16[64,256]{1,0:T(8,128)(2,1)S(1)} collective-permute-done((bf16[64,256]{1,0:T(8,128)(2,1)S(1)}, bf16[64,256]{1,0:T(8,128)(2,1)S(1)}, u32[]{:S(2)}, u32[]{:S(2)}) %collective-permute-start.4) | collective-permute-done | bytes 32800 | tf_op jit(solution)/shard_map/ppermute | solution.py:116
  16.9 0.0 copy-start.5
  16.9 0.0 copy-start.4
  16.9 0.1 collective-permute-start.7
  17.0 1.6 %collective-permute-start.6 = (bf16[64,256]{1,0:T(8,128)(2,1)S(1)}, bf16[64,256]{1,0:T(8,128)(2,1)S(1)}, u32[]{:S(2)}, u32[]{:S(2)}) collective-permute-start(bf16[64,256]{1,0:T(8,128)(2,1)S(1)} %add_convert_fusion.mine), channel_id=1, source_target_pairs={{0,16},{1,17},{2,18},{3,19},{4,20},{5,21},{6,22},{7,23},{8,24},{9,... | collective-permute-start | bytes 98312 | tf_op jit(solution)/shard_map/ppermute | solution.py:116
  18.6 0.3 %collective-permute-start.5 = (bf16[64,256]{1,0:T(8,128)(2,1)S(1)}, bf16[64,256]{1,0:T(8,128)(2,1)S(1)}, u32[]{:S(2)}, u32[]{:S(2)}) collective-permute-start(bf16[64,256]{1,0:T(8,128)(2,1)S(1)} %add_convert_fusion.mine), channel_id=1, source_target_pairs={{0,1},{1,0},{2,3},{3,2},{4,5},{5,4},{6,7},{7,6},{8,9},{9,8},{10,11... | collective-permute-start | bytes 98312 | tf_op jit(solution)/shard_map/ppermute | solution.py:116
  18.9 0.0 copy-done.5
  18.9 0.0 copy-done.1
  18.9 0.0 copy-done.2
  18.9 0.0 copy-done.4
  18.9 0.2 shard_map.112
  19.1 1.6 %collective-permute-done.7.both_piece = bf16[64,256]{1,0:T(8,128)(2,1)S(1)} collective-permute-done((bf16[64,256]{1,0:T(8,128)(2,1)S(1)}, bf16[64,256]{1,0:T(8,128)(2,1)S(1)}, u32[]{:S(2)}, u32[]{:S(2)}) %collective-permute-start.7) | collective-permute-done | bytes 32800 | tf_op jit(solution)/shard_map/ppermute | solution.py:116
  20.7 0.4 %collective-permute-done.6.tower_piece = bf16[64,256]{1,0:T(8,128)(2,1)S(1)} collective-permute-done((bf16[64,256]{1,0:T(8,128)(2,1)S(1)}, bf16[64,256]{1,0:T(8,128)(2,1)S(1)}, u32[]{:S(2)}, u32[]{:S(2)}) %collective-permute-start.6) | collective-permute-done | bytes 32800 | tf_op jit(solution)/shard_map/ppermute | solution.py:116
  21.1 0.0 collective-permute-done.5.side_piece
  21.1 1.8 %shard_map.113 = (f32[2,512,256]{2,1,0:T(8,128)}, bf16[2,64,512]{2,1,0:T(8,128)(2,1)}, f32[32,256]{1,0:T(8,128)}, f32[32,256]{1,0:T(8,128)}, f32[2,32]{1,0:T(2,128)}) custom-call(bf16[64,256]{1,0:T(8,128)(2,1)S(1)} %add_convert_fusion.mine, bf16[64,256]{1,0:T(8,128)(2,1)S(1)} %collective-permute-done.5.side_piece, ...), custom_call_target="tpu_custom_call" | custom-call | flops 167772160 | bytes 4194304 | tf_op jit(solution)/shard_map/pallas_call | solution.py:336
  (4 shorter events, 0.0 us)
Async XLA Ops:
  0.6 1.8 %copy-start = (bf16[2,512,256]{2,1,0:T(8,128)(2,1)S(1)}, bf16[2,512,256]{2,1,0:T(8,128)(2,1)}, u32[]{:S(2)}) copy-start(bf16[2,512,256]{2,1,0:T(8,128)(2,1)} %comp.3) | copy-start | bytes 1572868
  0.6 1.8 %copy-start.3 = (bf16[2,512,64]{1,2,0:T(8,128)(2,1)S(1)}, bf16[2,512,64]{1,2,0:T(8,128)(2,1)}, u32[]{:S(2)}) copy-start(bf16[2,512,64]{1,2,0:T(8,128)(2,1)} %param.7) | copy-start | bytes 393220
  1.9 1.4 %collective-permute-start = (f32[64,256]{1,0:T(8,128)S(1)}, f32[64,256]{1,0:T(8,128)S(1)}, u32[]{:S(2)}, u32[]{:S(2)}) collective-permute-start(f32[64,256]{1,0:T(8,128)S(1)} %shard_map.111), channel_id=1, source_target_pairs={{0,1},{1,0},{2,3},{3,2},{4,5},{5,4},{6,7},{7,6},{8,9},{9,8},{10,11... | collective-permute-start | bytes 196616 | tf_op jit(solution)/shard_map/ppermute | solution.py:116
  2.5 16.4 %copy-start.1 = (bf16[1024,256]{1,0:T(8,128)(2,1)S(1)}, bf16[1024,256]{1,0:T(8,128)(2,1)}, u32[]{:S(2)}) copy-start(bf16[1024,256]{1,0:T(8,128)(2,1)} %down.3) | copy-start | bytes 1572868
  2.5 16.4 %copy-start.2 = (bf16[1024,256]{1,0:T(8,128)(2,1)S(1)}, bf16[1024,256]{1,0:T(8,128)(2,1)}, u32[]{:S(2)}) copy-start(bf16[1024,256]{1,0:T(8,128)(2,1)} %upper.3) | copy-start | bytes 1572868
  3.4 6.4 %collective-permute-start.3 = (f32[64,256]{1,0:T(8,128)S(1)}, f32[64,256]{1,0:T(8,128)S(1)}, u32[]{:S(2)}, u32[]{:S(2)}) collective-permute-start(f32[64,256]{1,0:T(8,128)S(1)} %add.15), channel_id=1, source_target_pairs={{0,6},{1,7},{2,4},{3,5},{4,2},{5,3},{6,0},{7,1},{8,14},{9,15},{10,... | collective-permute-start | bytes 196616 | tf_op jit(solution)/shard_map/ppermute | solution.py:116
  7.3 4.3 %collective-permute-start.2 = (f32[64,256]{1,0:T(8,128)S(1)}, f32[64,256]{1,0:T(8,128)S(1)}, u32[]{:S(2)}, u32[]{:S(2)}) collective-permute-start(f32[64,256]{1,0:T(8,128)S(1)} %add.15), channel_id=1, source_target_pairs={{0,4},{1,5},{2,6},{3,7},{4,0},{5,1},{6,2},{7,3},{8,12},{9,13},{10,... | collective-permute-start | bytes 196616 | tf_op jit(solution)/shard_map/ppermute | solution.py:116
  7.8 4.3 %collective-permute-start.1 = (f32[64,256]{1,0:T(8,128)S(1)}, f32[64,256]{1,0:T(8,128)S(1)}, u32[]{:S(2)}, u32[]{:S(2)}) collective-permute-start(f32[64,256]{1,0:T(8,128)S(1)} %add.15), channel_id=1, source_target_pairs={{0,2},{1,3},{2,0},{3,1},{4,6},{5,7},{6,4},{7,5},{8,10},{9,11},{10,... | collective-permute-start | bytes 196616 | tf_op jit(solution)/shard_map/ppermute | solution.py:116
  12.0 4.9 %collective-permute-start.4 = (bf16[64,256]{1,0:T(8,128)(2,1)S(1)}, bf16[64,256]{1,0:T(8,128)(2,1)S(1)}, u32[]{:S(2)}, u32[]{:S(2)}) collective-permute-start(bf16[64,256]{1,0:T(8,128)(2,1)S(1)} %get-tuple-element.25), channel_id=1, source_target_pairs={{0,8},{1,9},{2,10},{3,11},{4,12},{5,13},{6,14},{7,15},{8,0},{9,1},... | collective-permute-start | bytes 98312 | tf_op jit(solution)/shard_map/ppermute | solution.py:116
  16.9 2.0 %copy-start.5 = (bf16[1024]{0:T(1024)(128)(2,1)S(1)}, bf16[1024]{0:T(1024)(128)(2,1)}, u32[]{:S(2)}) copy-start(bf16[1024]{0:T(1024)(128)(2,1)} %param.12) | copy-start | bytes 6148
  16.9 2.0 %copy-start.4 = (f32[1024]{0:T(1024)S(1)}, f32[1024]{0:T(1024)}, u32[]{:S(2)}) copy-start(f32[1024]{0:T(1024)} %param.11) | copy-start | bytes 12292
  16.9 3.7 %collective-permute-start.7 = (bf16[64,256]{1,0:T(8,128)(2,1)S(1)}, bf16[64,256]{1,0:T(8,128)(2,1)S(1)}, u32[]{:S(2)}, u32[]{:S(2)}) collective-permute-start(bf16[64,256]{1,0:T(8,128)(2,1)S(1)} %add_convert_fusion.mine), channel_id=1, source_target_pairs={{0,17},{1,16},{2,19},{3,18},{4,21},{5,20},{6,23},{7,22},{8,25},{9,... | collective-permute-start | bytes 98312 | tf_op jit(solution)/shard_map/ppermute | solution.py:116
  17.0 4.0 %collective-permute-start.6 = (bf16[64,256]{1,0:T(8,128)(2,1)S(1)}, bf16[64,256]{1,0:T(8,128)(2,1)S(1)}, u32[]{:S(2)}, u32[]{:S(2)}) collective-permute-start(bf16[64,256]{1,0:T(8,128)(2,1)S(1)} %add_convert_fusion.mine), channel_id=1, source_target_pairs={{0,16},{1,17},{2,18},{3,19},{4,20},{5,21},{6,22},{7,23},{8,24},{9,... | collective-permute-start | bytes 98312 | tf_op jit(solution)/shard_map/ppermute | solution.py:116
  18.6 2.5 %collective-permute-start.5 = (bf16[64,256]{1,0:T(8,128)(2,1)S(1)}, bf16[64,256]{1,0:T(8,128)(2,1)S(1)}, u32[]{:S(2)}, u32[]{:S(2)}) collective-permute-start(bf16[64,256]{1,0:T(8,128)(2,1)S(1)} %add_convert_fusion.mine), channel_id=1, source_target_pairs={{0,1},{1,0},{2,3},{3,2},{4,5},{5,4},{6,7},{7,6},{8,9},{9,8},{10,11... | collective-permute-start | bytes 98312 | tf_op jit(solution)/shard_map/ppermute | solution.py:116
